TPU v7x, 32 devices: a whole 2x2x4 slice. The times are simulated.
32 devices in a mesh: pipe: 2 (over x), dp: 16 (over z, y, core).
Axes of the slice: x: 2, y: 2, z: 4, core: 2. Of those that a mesh axis runs over, the one named last changes fastest.
Arguments:
- samples: bfloat16 [80, 3, 32, 640], P('dp'), may hold values from -6 to 6
- timesteps: int32 [80], P('dp'), may hold values from 0 to 999
- cotangent: bfloat16 [80, 3, 32, 640], P('dp'), may hold values from -0.059814453 to 0.059814453
- spatial_weight: bfloat16 [2, 5760, 640], P('pipe', 'dp'), may hold values from -0.078125 to 0.078125
- temporal_weight: bfloat16 [2, 1920, 640], P('pipe', 'dp'), may hold values from -0.125 to 0.125
Outputs:
- spatial_grad: float32 [2, 5760, 640], P('pipe', 'dp')
- temporal_grad: float32 [2, 1920, 640], P('pipe', 'dp')
All inputs are finite; a program needn't handle non-finite values.
Results may differ from a plain program's by a relative error of at most 0.034.
Values may be sent and summed in bfloat16 or wider, within the bound.
No kernel may reach another device: no remote copies, remote signals or barrier semaphores. Data moves between devices by JAX's collectives and lax.ppermute only.
A program may use at most 128 MiB of HBM per device.

v0:
```python
import math

import jax
import jax.numpy as jnp
from jax import lax
from jax.sharding import PartitionSpec as P

HEIGHT = 8
WIDTH = 4


def passed_along(value, axis, steps):
    count = lax.axis_size(axis)
    first, last = (max(0, -steps), min(count, count - steps))
    return lax.ppermute(value, axis, [(source, source + steps) for source in range(first, last)])


def embedding_of(step, channels):
    half_width = channels // 2
    frequency = jnp.exp(-math.log(10000.0) * jnp.arange(half_width, dtype=jnp.float32) / half_width)
    phases = step.astype(jnp.float32) * frequency
    return jnp.concatenate([jnp.sin(phases), jnp.cos(phases)])


def normalize(summed):
    return summed * lax.rsqrt(jnp.mean(summed * summed, axis=-1, keepdims=True) + 1e-06)


def spatial_columns(normed):
    frames, pixels, channels = normed.shape
    grid = normed.reshape(frames, HEIGHT, WIDTH, channels)
    padded = jnp.pad(grid, ((0, 0), (1, 1), (1, 1), (0, 0)))
    pieces = [
        padded[:, row : row + HEIGHT, col : col + WIDTH, :] for row in range(3) for col in range(3)
    ]
    return jnp.concatenate(pieces, axis=-1).reshape(frames * pixels, 9 * channels)


def spatial_fold(grads, frames, channels):
    parts = grads.reshape(frames, HEIGHT, WIDTH, 9, channels)
    padded = jnp.zeros((frames, HEIGHT + 2, WIDTH + 2, channels), jnp.float32)
    for row in range(3):
        for col in range(3):
            padded = padded.at[:, row : row + HEIGHT, col : col + WIDTH, :].add(
                parts[:, :, :, row * 3 + col, :]
            )
    return padded[:, 1 : HEIGHT + 1, 1 : WIDTH + 1, :].reshape(frames, HEIGHT * WIDTH, channels)


def temporal_columns(activated):
    frames, pixels, channels = activated.shape
    padded = jnp.pad(activated, ((1, 1), (0, 0), (0, 0)))
    pieces = [padded[tap : tap + frames] for tap in range(3)]
    return jnp.concatenate(pieces, axis=-1).reshape(frames * pixels, 3 * channels)


def temporal_fold(grads, frames, pixels, channels):
    parts = grads.reshape(frames, pixels, 3, channels)
    padded = jnp.zeros((frames + 2, pixels, channels), jnp.float32)
    for tap in range(3):
        padded = padded.at[tap : tap + frames].add(parts[:, :, tap, :])
    return padded[1 : frames + 1]


def section_forward(block_in, embedding, spatial, temporal):
    frames, pixels, channels = block_in.shape
    summed = block_in.astype(jnp.float32) + embedding
    normed = normalize(summed).astype(jnp.bfloat16)
    preact = jnp.dot(spatial_columns(normed), spatial, preferred_element_type=jnp.float32)
    activated = jax.nn.silu(preact).astype(jnp.bfloat16).reshape(frames, pixels, channels)
    mixed = jnp.dot(temporal_columns(activated), temporal, preferred_element_type=jnp.float32)
    return (block_in.astype(jnp.float32) + mixed.reshape(frames, pixels, channels)).astype(
        jnp.bfloat16
    )


def backward_first(block_in, embedding, spatial, temporal, upstream):
    frames, pixels, channels = block_in.shape
    summed = block_in.astype(jnp.float32) + embedding
    normed = normalize(summed).astype(jnp.bfloat16)
    columns = spatial_columns(normed)
    preact = jnp.dot(columns, spatial, preferred_element_type=jnp.float32)
    activated = jax.nn.silu(preact).astype(jnp.bfloat16).reshape(frames, pixels, channels)
    tcolumns = temporal_columns(activated)
    upstream_flat = upstream.reshape(frames * pixels, channels)
    temporal_term = jnp.dot(tcolumns.T, upstream_flat, preferred_element_type=jnp.float32)
    act_grad = temporal_fold(
        jnp.dot(upstream_flat, temporal.T, preferred_element_type=jnp.float32),
        frames,
        pixels,
        channels,
    )
    logistic = jax.nn.sigmoid(preact)
    slope = logistic * (1.0 + preact * (1.0 - logistic))
    pre_grad = (act_grad.reshape(frames * pixels, channels) * slope).astype(jnp.bfloat16)
    return (temporal_term, pre_grad, columns)


def backward_second(block_in, embedding, spatial, upstream, pre_grad, columns):
    frames, pixels, channels = block_in.shape
    summed = block_in.astype(jnp.float32) + embedding
    spatial_term = jnp.dot(columns.T, pre_grad, preferred_element_type=jnp.float32)
    norm_grad = spatial_fold(
        jnp.dot(pre_grad, spatial.T, preferred_element_type=jnp.float32), frames, channels
    )
    _, pullback = jax.vjp(normalize, summed)
    back_input = (upstream.astype(jnp.float32) + pullback(norm_grad)[0]).astype(jnp.bfloat16)
    return (back_input, spatial_term)


def section_backward(block_in, embedding, spatial, temporal, upstream):
    temporal_term, pre_grad, columns = backward_first(
        block_in, embedding, spatial, temporal, upstream
    )
    back_input, spatial_term = backward_second(
        block_in, embedding, spatial, upstream, pre_grad, columns
    )
    return (back_input, spatial_term, temporal_term)


def per_device(samples, timesteps, cotangent, spatial_weight, temporal_weight):
    sections = lax.axis_size("pipe")
    section_index = lax.axis_index("pipe")
    micro_count = samples.shape[0]
    frames, pixels, channels = (samples.shape[1], samples.shape[2], samples.shape[3])
    moments = jnp.arange(micro_count + sections - 1, dtype=jnp.int32)
    blank = jnp.zeros((frames, pixels, channels), jnp.bfloat16)
    full_spatial, full_temporal = (
        lax.all_gather(spatial_weight[0], "dp", axis=0, tiled=True),
        lax.all_gather(temporal_weight[0], "dp", axis=0, tiled=True),
    )

    def forward_step(carry, moment):
        incoming, stash = carry
        position = moment - section_index
        active = (position >= 0) & (position < micro_count)
        picked = jnp.clip(position, 0, micro_count - 1)
        own = lax.dynamic_index_in_dim(samples, picked, 0, keepdims=False)
        embedding = embedding_of(
            lax.dynamic_index_in_dim(timesteps, picked, 0, keepdims=False), channels
        )
        block_in = jnp.where(section_index == 0, own, incoming)
        result = lax.cond(
            active & (section_index < sections - 1),
            lambda: section_forward(block_in, embedding, full_spatial, full_temporal),
            lambda: blank,
        )
        stash = jnp.where(
            active, lax.dynamic_update_index_in_dim(stash, block_in, picked, 0), stash
        )
        passed = passed_along(result, "pipe", 1)
        return ((passed, stash), None)

    (_, stash), _ = lax.scan(forward_step, (blank, jnp.zeros_like(samples)), moments)
    back_spatial, back_temporal = (full_spatial, full_temporal)

    def inputs_at(moment, incoming):
        position = moment - (sections - 1 - section_index)
        active = (position >= 0) & (position < micro_count)
        picked = jnp.clip(position, 0, micro_count - 1)
        block_in = lax.dynamic_index_in_dim(stash, picked, 0, keepdims=False)
        embedding = embedding_of(
            lax.dynamic_index_in_dim(timesteps, picked, 0, keepdims=False), channels
        )
        given = lax.dynamic_index_in_dim(cotangent, picked, 0, keepdims=False)
        upstream = jnp.where(section_index == sections - 1, given, incoming)
        return (active, block_in, embedding, upstream)

    def backward_step(carry, moment):
        incoming, grad_spatial, grad_temporal = carry
        active, block_in, embedding, upstream = inputs_at(moment, incoming)

        def working():
            back_input, spatial_term, temporal_term = section_backward(
                block_in, embedding, back_spatial, back_temporal, upstream
            )
            return (back_input, grad_spatial + spatial_term, grad_temporal + temporal_term)

        def waiting():
            return (blank, grad_spatial, grad_temporal)

        back_input, grad_spatial, grad_temporal = lax.cond(active, working, waiting)
        passed = passed_along(back_input, "pipe", -1)
        return ((passed, grad_spatial, grad_temporal), None)

    start = (
        blank,
        jnp.zeros(back_spatial.shape, jnp.float32),
        jnp.zeros(back_temporal.shape, jnp.float32),
    )
    (_, grad_spatial, grad_temporal), _ = lax.scan(backward_step, start, moments)
    share_spatial, share_temporal = (
        lax.psum_scatter(
            grad_spatial.astype(jnp.bfloat16).astype(jnp.float32).astype(jnp.bfloat16),
            "dp",
            scatter_dimension=0,
            tiled=True,
        ).astype(jnp.float32),
        lax.psum_scatter(
            grad_temporal.astype(jnp.bfloat16).astype(jnp.float32).astype(jnp.bfloat16),
            "dp",
            scatter_dimension=0,
            tiled=True,
        ).astype(jnp.float32),
    )
    return (share_spatial[None], share_temporal[None])


def solution(mesh):
    return jax.shard_map(
        per_device,
        mesh=mesh,
        in_specs=(
            P("dp", None, None, None),
            P("dp"),
            P("dp", None, None, None),
            P("pipe", "dp", None),
            P("pipe", "dp", None),
        ),
        out_specs=(P("pipe", "dp", None), P("pipe", "dp", None)),
        check_vma=False,
    )
```

profile of v0, /device:TPU:0, one launch (start us, length us, event | category | flops | bytes accessed | tf_op | source)
XLA Modules:
  0.0 989.7 jit_solution(5752250918087115683)
XLA Ops:
  8.7 46.8 %all-gather.5.cloned.1.call-done = bf16[1,1920,640]{2,1,0:T(8,128)(2,1)} async-done(((bf16[1,120,640]{2,1,0:T(8,128)(2,1)}), bf16[1,1920,640]{2,1,0:T(8,128)(2,1)}) %all-gather.5.cloned.1.call-update) | async-done | bytes 2457616 | tf_op jit(solution)/shard_map/all_gather | solution.py:130
  55.5 69.5 %all-gather.7.cloned.1.call-done = bf16[1,5760,640]{2,1,0:T(8,128)(2,1)} async-done(((bf16[1,360,640]{2,1,0:T(8,128)(2,1)}), bf16[1,5760,640]{2,1,0:T(8,128)(2,1)}) %all-gather.7.cloned.1.call-update) | async-done | bytes 7372816 | tf_op jit(solution)/shard_map/all_gather | solution.py:129
  125.9 96.0 %while.42 = (s32[]{:T(128)}, bf16[3,32,640]{2,1,0:T(8,128)(2,1)S(1)}, bf16[5,3,32,640]{3,2,1,0:T(8,128)(2,1)}, s32[6]{0:T(128)S(1)}, s32[]{:T(128)}, /*index=5*/...) while((s32[]{:T(128)}, ...), condition=%wide.region_4.5_spmd, body=%wide.region_0.4_spmd.sunk | while | flops 945931648 | bytes 19061576 | solution.py:154
  130.9 7.9 conditional.4
  132.0 4.5 multiply_convert_fusion
  140.1 3.3 collective-permute-done
  148.3 7.8 conditional.4
  149.4 4.5 multiply_convert_fusion
  165.3 7.8 conditional.4
  166.4 4.5 multiply_convert_fusion
  181.9 7.9 conditional.4
  182.9 4.5 multiply_convert_fusion
  198.5 7.9 conditional.4
  199.5 4.5 multiply_convert_fusion
  215.1 4.3 collective-permute-start
  225.1 6.2 broadcast_in_dim.49
  231.2 589.0 %while.43 = (s32[]{:T(128)}, bf16[3,32,640]{2,1,0:T(8,128)(2,1)S(1)}, f32[5760,640]{1,0:T(8,128)}, f32[1920,640]{1,0:T(8,128)}, s32[6]{0:T(128)}, /*index=5*/s32...) while((s32[]{:T(128)}, ...), condition=%wide.region_11.12_spmd, body=%wide.region_5.11_spmd.sunk | while | flops 2604136192 | bytes 131155824 | solution.py:191
  237.1 92.1 %collective-permute-done.1 = bf16[3,32,640]{2,1,0:T(8,128)(2,1)S(1)} collective-permute-done((bf16[3,32,640]{2,1,0:T(8,128)(2,1)}, bf16[3,32,640]{2,1,0:T(8,128)(2,1)S(1)}, u32[]{:S(2)}, u32[]{:S(2)}) %collective-permute-start.1) | collective-permute-done | bytes 122912 | tf_op jit(solution)/shard_map/while/body/eval_jaxpr/ppermute | solution.py:15
  333.2 87.3 %conditional.5 = (bf16[3,32,640]{2,1,0:T(8,128)(2,1)}, f32[5760,640]{1,0:T(8,128)}, f32[1920,640]{1,0:T(8,128)}) conditional(s32[]{:T(128)} %convert_element_type.150, (f32[5760,640]{1,0:T(8,128)}, f32[1920,640]{1,0:T(8,128)}) %tuple.162, (pred[]{:T(512)}, bf16[5,3,32,640]{3,2,1,0:T(8,128)(2,1)}, s32[]{:T(128)}, bf16[3,32,640]{2,1,0:T(8,128)(2,1)S(1)}, ...), branch_computations={%region_6.6_spmd, %region_7.10_spmd} | conditional | flops 2604134912 | bytes 130656240 | solution.py:182
  361.4 4.9 multiply_convert_fusion.1
  366.4 3.6 fusion.47
  370.7 3.5 reshape.636
  374.2 10.0 %fusion.44 = (f32[3,8,4,1,640]{4,3,2,1,0:T(1,128)S(1)}, f32[3,8,4,1,640]{4,3,2,1,0:T(1,128)S(1)}, f32[3,8,4,1,640]{4,3,2,1,0:T(1,128)S(1)}, f32[3,8,4,1,640]{4,3...) fusion(f32[3,8,4,9,640]{4,3,2,1,0:T(8,128)} %reshape.636), kind=kLoop, calls=%fused_computation.124 | loop fusion | bytes 4423680 | tf_op jit(solution)/shard_map/while/body/eval_jaxpr/cond/branch_1_fun/slice | solution.py:45
  385.7 2.8 scatter-add.26
  402.4 5.6 bitcast_add_fusion
  407.9 12.5 %convolution_add_fusion = f32[5760,640]{1,0:T(8,128)} fusion(f32[5760,640]{1,0:T(8,128)} %get-tuple-element.507, bf16[96,5760]{1,0:T(8,128)(2,1)S(1)} %copy-done.1, bf16[96,640]{1,0:T(8,128)(2,1)S(1)} %get-tuple-element.603), kind=kOutput, calls=%fused_computation.43 | convolution fusion | flops 711475200 | bytes 30720000 | tf_op jit(solution)/shard_map/while/body/eval_jaxpr/cond/branch_1_fun/dot_general | solution.py:102
  421.8 5.7 collective-permute-done.1
  431.4 87.3 %conditional.5 = (bf16[3,32,640]{2,1,0:T(8,128)(2,1)}, f32[5760,640]{1,0:T(8,128)}, f32[1920,640]{1,0:T(8,128)}) conditional(s32[]{:T(128)} %convert_element_type.150, (f32[5760,640]{1,0:T(8,128)}, f32[1920,640]{1,0:T(8,128)}) %tuple.162, (pred[]{:T(512)}, bf16[5,3,32,640]{3,2,1,0:T(8,128)(2,1)}, s32[]{:T(128)}, bf16[3,32,640]{2,1,0:T(8,128)(2,1)S(1)}, ...), branch_computations={%region_6.6_spmd, %region_7.10_spmd} | conditional | flops 2604134912 | bytes 130656240 | solution.py:182
  459.6 4.9 multiply_convert_fusion.1
  464.6 3.6 fusion.47
  468.9 3.5 reshape.636
  472.4 10.0 %fusion.44 = (f32[3,8,4,1,640]{4,3,2,1,0:T(1,128)S(1)}, f32[3,8,4,1,640]{4,3,2,1,0:T(1,128)S(1)}, f32[3,8,4,1,640]{4,3,2,1,0:T(1,128)S(1)}, f32[3,8,4,1,640]{4,3...) fusion(f32[3,8,4,9,640]{4,3,2,1,0:T(8,128)} %reshape.636), kind=kLoop, calls=%fused_computation.124 | loop fusion | bytes 4423680 | tf_op jit(solution)/shard_map/while/body/eval_jaxpr/cond/branch_1_fun/slice | solution.py:45
  483.9 2.8 scatter-add.26
  500.6 5.6 bitcast_add_fusion
  506.2 12.5 %convolution_add_fusion = f32[5760,640]{1,0:T(8,128)} fusion(f32[5760,640]{1,0:T(8,128)} %get-tuple-element.507, bf16[96,5760]{1,0:T(8,128)(2,1)S(1)} %copy-done.1, bf16[96,640]{1,0:T(8,128)(2,1)S(1)} %get-tuple-element.603), kind=kOutput, calls=%fused_computation.43 | convolution fusion | flops 711475200 | bytes 30720000 | tf_op jit(solution)/shard_map/while/body/eval_jaxpr/cond/branch_1_fun/dot_general | solution.py:102
  520.0 5.7 collective-permute-done.1
  529.6 87.3 %conditional.5 = (bf16[3,32,640]{2,1,0:T(8,128)(2,1)}, f32[5760,640]{1,0:T(8,128)}, f32[1920,640]{1,0:T(8,128)}) conditional(s32[]{:T(128)} %convert_element_type.150, (f32[5760,640]{1,0:T(8,128)}, f32[1920,640]{1,0:T(8,128)}) %tuple.162, (pred[]{:T(512)}, bf16[5,3,32,640]{3,2,1,0:T(8,128)(2,1)}, s32[]{:T(128)}, bf16[3,32,640]{2,1,0:T(8,128)(2,1)S(1)}, ...), branch_computations={%region_6.6_spmd, %region_7.10_spmd} | conditional | flops 2604134912 | bytes 130656240 | solution.py:182
  557.8 4.9 multiply_convert_fusion.1
  562.8 3.6 fusion.47
  567.1 3.5 reshape.636
  570.6 10.0 %fusion.44 = (f32[3,8,4,1,640]{4,3,2,1,0:T(1,128)S(1)}, f32[3,8,4,1,640]{4,3,2,1,0:T(1,128)S(1)}, f32[3,8,4,1,640]{4,3,2,1,0:T(1,128)S(1)}, f32[3,8,4,1,640]{4,3...) fusion(f32[3,8,4,9,640]{4,3,2,1,0:T(8,128)} %reshape.636), kind=kLoop, calls=%fused_computation.124 | loop fusion | bytes 4423680 | tf_op jit(solution)/shard_map/while/body/eval_jaxpr/cond/branch_1_fun/slice | solution.py:45
  598.8 5.6 bitcast_add_fusion
  604.3 12.5 %convolution_add_fusion = f32[5760,640]{1,0:T(8,128)} fusion(f32[5760,640]{1,0:T(8,128)} %get-tuple-element.507, bf16[96,5760]{1,0:T(8,128)(2,1)S(1)} %copy-done.1, bf16[96,640]{1,0:T(8,128)(2,1)S(1)} %get-tuple-element.603), kind=kOutput, calls=%fused_computation.43 | convolution fusion | flops 711475200 | bytes 30720000 | tf_op jit(solution)/shard_map/while/body/eval_jaxpr/cond/branch_1_fun/dot_general | solution.py:102
  618.2 5.7 collective-permute-done.1
  627.8 87.3 %conditional.5 = (bf16[3,32,640]{2,1,0:T(8,128)(2,1)}, f32[5760,640]{1,0:T(8,128)}, f32[1920,640]{1,0:T(8,128)}) conditional(s32[]{:T(128)} %convert_element_type.150, (f32[5760,640]{1,0:T(8,128)}, f32[1920,640]{1,0:T(8,128)}) %tuple.162, (pred[]{:T(512)}, bf16[5,3,32,640]{3,2,1,0:T(8,128)(2,1)}, s32[]{:T(128)}, bf16[3,32,640]{2,1,0:T(8,128)(2,1)S(1)}, ...), branch_computations={%region_6.6_spmd, %region_7.10_spmd} | conditional | flops 2604134912 | bytes 130656240 | solution.py:182
  656.0 4.9 multiply_convert_fusion.1
  661.0 3.6 fusion.47
  665.3 3.5 reshape.636
  668.8 10.0 %fusion.44 = (f32[3,8,4,1,640]{4,3,2,1,0:T(1,128)S(1)}, f32[3,8,4,1,640]{4,3,2,1,0:T(1,128)S(1)}, f32[3,8,4,1,640]{4,3,2,1,0:T(1,128)S(1)}, f32[3,8,4,1,640]{4,3...) fusion(f32[3,8,4,9,640]{4,3,2,1,0:T(8,128)} %reshape.636), kind=kLoop, calls=%fused_computation.124 | loop fusion | bytes 4423680 | tf_op jit(solution)/shard_map/while/body/eval_jaxpr/cond/branch_1_fun/slice | solution.py:45
  697.0 5.6 bitcast_add_fusion
  702.5 12.5 %convolution_add_fusion = f32[5760,640]{1,0:T(8,128)} fusion(f32[5760,640]{1,0:T(8,128)} %get-tuple-element.507, bf16[96,5760]{1,0:T(8,128)(2,1)S(1)} %copy-done.1, bf16[96,640]{1,0:T(8,128)(2,1)S(1)} %get-tuple-element.603), kind=kOutput, calls=%fused_computation.43 | convolution fusion | flops 711475200 | bytes 30720000 | tf_op jit(solution)/shard_map/while/body/eval_jaxpr/cond/branch_1_fun/dot_general | solution.py:102
  716.4 5.7 collective-permute-done.1
  726.0 87.3 %conditional.5 = (bf16[3,32,640]{2,1,0:T(8,128)(2,1)}, f32[5760,640]{1,0:T(8,128)}, f32[1920,640]{1,0:T(8,128)}) conditional(s32[]{:T(128)} %convert_element_type.150, (f32[5760,640]{1,0:T(8,128)}, f32[1920,640]{1,0:T(8,128)}) %tuple.162, (pred[]{:T(512)}, bf16[5,3,32,640]{3,2,1,0:T(8,128)(2,1)}, s32[]{:T(128)}, bf16[3,32,640]{2,1,0:T(8,128)(2,1)S(1)}, ...), branch_computations={%region_6.6_spmd, %region_7.10_spmd} | conditional | flops 2604134912 | bytes 130656240 | solution.py:182
  754.2 4.9 multiply_convert_fusion.1
  759.2 3.6 fusion.47
  763.5 3.5 reshape.636
  767.0 10.0 %fusion.44 = (f32[3,8,4,1,640]{4,3,2,1,0:T(1,128)S(1)}, f32[3,8,4,1,640]{4,3,2,1,0:T(1,128)S(1)}, f32[3,8,4,1,640]{4,3,2,1,0:T(1,128)S(1)}, f32[3,8,4,1,640]{4,3...) fusion(f32[3,8,4,9,640]{4,3,2,1,0:T(8,128)} %reshape.636), kind=kLoop, calls=%fused_computation.124 | loop fusion | bytes 4423680 | tf_op jit(solution)/shard_map/while/body/eval_jaxpr/cond/branch_1_fun/slice | solution.py:45
  795.2 5.6 bitcast_add_fusion
  800.7 12.5 %convolution_add_fusion = f32[5760,640]{1,0:T(8,128)} fusion(f32[5760,640]{1,0:T(8,128)} %get-tuple-element.507, bf16[96,5760]{1,0:T(8,128)(2,1)S(1)} %copy-done.1, bf16[96,640]{1,0:T(8,128)(2,1)S(1)} %get-tuple-element.603), kind=kOutput, calls=%fused_computation.43 | convolution fusion | flops 711475200 | bytes 30720000 | tf_op jit(solution)/shard_map/while/body/eval_jaxpr/cond/branch_1_fun/dot_general | solution.py:102
  814.6 5.7 collective-permute-done.1
  820.2 4.1 convert_element_type.117
  824.4 9.1 convert_element_type.116
  833.6 51.6 %reduce-scatter.9.cloned.1.call-done = bf16[120,640]{1,0:T(8,128)(2,1)} async-done(((bf16[1920,640]{1,0:T(8,128)(2,1)}), bf16[120,640]{1,0:T(8,128)(2,1)}) %reduce-scatter.9.cloned.1.call-update) | async-done | bytes 153616
  886.8 94.4 %reduce-scatter.7.cloned.1.call-done = bf16[360,640]{1,0:T(8,128)(2,1)} async-done(((bf16[5760,640]{1,0:T(8,128)(2,1)}), bf16[360,640]{1,0:T(8,128)(2,1)}) %reduce-scatter.7.cloned.1.call-update) | async-done | bytes 460816
  (668 shorter events, 319.9 us)
Async XLA Ops:
  7.2 48.4 %all-gather.5.cloned.1.call-start = ((), (), s32[]{:S(2)}) async-start(), calls=%async_computation.2 | async-start | bytes 2611200 | tf_op jit(solution)/shard_map/all_gather | solution.py:130
  7.9 117.1 %all-gather.7.cloned.1.call-start = ((), (), s32[]{:S(2)}) async-start(), calls=%async_computation.3 | async-start | bytes 7833600 | tf_op jit(solution)/shard_map/all_gather | solution.py:129
  8.6 876.5 %reduce-scatter.9.cloned.1.call-start = ((), (), s32[]{:S(2)}) async-start(), calls=%async_computation.5 | async-start | bytes 2611200
  138.8 4.6 collective-permute-start
  156.2 4.1 collective-permute-start
  173.1 3.7 collective-permute-start
  189.8 3.7 collective-permute-start
  206.4 3.7 collective-permute-start
  215.1 6.8 collective-permute-start
  235.8 93.4 %collective-permute-start.1 = (bf16[3,32,640]{2,1,0:T(8,128)(2,1)}, bf16[3,32,640]{2,1,0:T(8,128)(2,1)S(1)}, u32[]{:S(2)}, u32[]{:S(2)}) collective-permute-start(bf16[3,32,640]{2,1,0:T(8,128)(2,1)} %get-tuple-element.777), channel_id=1, source_target_pairs={{16,0},{17,1},{18,2},{19,3},{20,4},{21,5},{22,6},{23,7},{24,8},{25... | collective-permute-start | bytes 368648 | tf_op jit(solution)/shard_map/while/body/eval_jaxpr/ppermute | solution.py:15
  336.9 4.2 copy-start.12
  343.1 23.2 %slice-start = ((s8[7372800]{0:T(1024)(128)(4,1)}), s8[3178496]{0:T(1024)(128)(4,1)S(1)}, s32[]{:S(2)}) async-start(s8[7372800]{0:T(1024)(128)(4,1)} %bitcast.136), calls=%async_computation.6 | async-start | bytes 6356992 | tf_op jit(solution)/shard_map/while/body/eval_jaxpr/cond
  356.4 4.8 copy-start.11
  356.5 4.8 copy-start.10
  356.5 4.8 copy-start.9
  356.5 4.9 copy-start.6
  361.4 5.0 copy-start
  361.4 5.0 slice-start.1
  366.3 3.6 copy-start.2
  402.3 5.6 copy-start.1
  420.5 7.0 collective-permute-start.1
  435.2 4.2 copy-start.12
  441.4 23.2 %slice-start = ((s8[7372800]{0:T(1024)(128)(4,1)}), s8[3178496]{0:T(1024)(128)(4,1)S(1)}, s32[]{:S(2)}) async-start(s8[7372800]{0:T(1024)(128)(4,1)} %bitcast.136), calls=%async_computation.6 | async-start | bytes 6356992 | tf_op jit(solution)/shard_map/while/body/eval_jaxpr/cond
  454.7 4.8 copy-start.11
  454.7 4.8 copy-start.10
  454.7 4.8 copy-start.9
  454.7 4.9 copy-start.6
  459.6 5.0 copy-start
  459.6 5.0 slice-start.1
  464.5 3.6 copy-start.2
  500.6 5.6 copy-start.1
  518.7 7.0 collective-permute-start.1
  533.4 4.2 copy-start.12
  539.6 23.2 %slice-start = ((s8[7372800]{0:T(1024)(128)(4,1)}), s8[3178496]{0:T(1024)(128)(4,1)S(1)}, s32[]{:S(2)}) async-start(s8[7372800]{0:T(1024)(128)(4,1)} %bitcast.136), calls=%async_computation.6 | async-start | bytes 6356992 | tf_op jit(solution)/shard_map/while/body/eval_jaxpr/cond
  552.9 4.8 copy-start.11
  552.9 4.8 copy-start.10
  552.9 4.8 copy-start.9
  552.9 4.9 copy-start.6
  557.8 5.0 copy-start
  557.8 5.0 slice-start.1
  598.7 5.6 copy-start.1
  616.9 7.0 collective-permute-start.1
  631.6 4.2 copy-start.12
  637.8 23.2 %slice-start = ((s8[7372800]{0:T(1024)(128)(4,1)}), s8[3178496]{0:T(1024)(128)(4,1)S(1)}, s32[]{:S(2)}) async-start(s8[7372800]{0:T(1024)(128)(4,1)} %bitcast.136), calls=%async_computation.6 | async-start | bytes 6356992 | tf_op jit(solution)/shard_map/while/body/eval_jaxpr/cond
  651.1 4.8 copy-start.11
  651.1 4.8 copy-start.10
  651.1 4.8 copy-start.9
  651.1 4.9 copy-start.6
  656.0 5.0 copy-start
  656.0 5.0 slice-start.1
  660.9 3.6 copy-start.2
  696.9 5.6 copy-start.1
  715.1 7.0 collective-permute-start.1
  729.8 4.2 copy-start.12
  736.0 23.2 %slice-start = ((s8[7372800]{0:T(1024)(128)(4,1)}), s8[3178496]{0:T(1024)(128)(4,1)S(1)}, s32[]{:S(2)}) async-start(s8[7372800]{0:T(1024)(128)(4,1)} %bitcast.136), calls=%async_computation.6 | async-start | bytes 6356992 | tf_op jit(solution)/shard_map/while/body/eval_jaxpr/cond
  749.3 4.8 copy-start.11
  749.3 4.8 copy-start.10
  749.3 4.8 copy-start.9
  749.3 4.9 copy-start.6
  754.2 5.0 copy-start
  754.2 5.0 slice-start.1
  795.1 5.6 copy-start.1
  813.3 7.0 collective-permute-start.1
  824.4 156.8 %reduce-scatter.7.cloned.1.call-start = ((), (), s32[]{:S(2)}) async-start(), calls=%async_computation.4 | async-start | bytes 7833600
  (32 other events, 94.2 us)
Sparse Core Ops, SparseCore 0:
  10.2 45.3 all-gather.4
  57.7 67.2 all-gather.6
  824.5 60.5 reduce-scatter.8
  889.1 92.0 reduce-scatter.6
where the time goes:
time: 994 us; the launch traced here: 990 us
  waiting for transfers between devices  400 us (40%)
  local copies, waits for them, and re-layouts  271 us (27%)
  matrix products  180 us (18%)
  other arithmetic  87.9 us (9%)
  starting transfers between devices  18.7 us (2%)
  loops' own time  18.3 us (2%)
  between operations  13.8 us (1%)
    unnamed x6, waiting for transfers between devices  147 us
    ppermute x12, waiting for transfers between devices, passed_along(): lax.ppermute(value, axis, [(source, source + steps) for source in range(f...  136 us
    all_gather x1, waiting for transfers between devices, per_device(): lax.all_gather(spatial_weight[0], 'dp', axis=0, tiled=True)  69.5 us
    dot_general x5, matrix products, backward_second(): jnp.dot(columns.T, pre_grad, preferred_element_type=jnp.float32)  62.6 us
    concatenate x90, local copies, waits for them, and re-layouts, spatial_columns(): jnp.concatenate(pieces, axis=-1).reshape(frames * pixels, 9 * channels)  61.9 us
    scatter-add x35, local copies, waits for them, and re-layouts, spatial_fold(): padded.at[:, row:row + HEIGHT, col:col + WIDTH, :]  58.2 us
    slice x5, local copies, waits for them, and re-layouts, spatial_fold(): parts[:, :, :, row * 3 + col, :]  49.9 us
    all_gather x1, waiting for transfers between devices, per_device(): lax.all_gather(temporal_weight[0], 'dp', axis=0, tiled=True)  46.8 us
  transfers between devices with their start and end apart: 16, of which 16 were waited for; matrix products, arithmetic and copies ran while one was open for 1% of the time, Pallas kernels for 0%

commit v1 on v0

--- a/solution.py
+++ b/solution.py
@@ -1,12 +1,19 @@
+import functools
 import math
 
 import jax
 import jax.numpy as jnp
 from jax import lax
+from jax.experimental import pallas as pl
+from jax.experimental.pallas import tpu as pltpu
 from jax.sharding import PartitionSpec as P
 
 HEIGHT = 8
 WIDTH = 4
+F32 = jnp.float32
+BF16 = jnp.bfloat16
+GRID = (4, 2, 2)
+LANES = 128
 
 
 def passed_along(value, axis, steps):
@@ -206,9 +213,420 @@
     return (share_spatial[None], share_temporal[None])
 
 
+def coordinates():
+    index = lax.axis_index("dp")
+    return index // (GRID[1] * GRID[2]), (index // GRID[2]) % GRID[1], index % GRID[2]
+
+
+def shifted(value, dz=0, dy=0, dc=0):
+    pairs = []
+    for z in range(GRID[0]):
+        for y in range(GRID[1]):
+            for c in range(GRID[2]):
+                place = ((z + dz) % GRID[0], (y + dy) % GRID[1], (c + dc) % GRID[2])
+                pairs.append(
+                    (
+                        (z * GRID[1] + y) * GRID[2] + c,
+                        (place[0] * GRID[1] + place[1]) * GRID[2] + place[2],
+                    )
+                )
+    return lax.ppermute(value, "dp", pairs)
+
+
+def swapped(value):
+    return lax.ppermute(value, "pipe", [(0, 1), (1, 0)])
+
+
+def part_of(value, index, axis):
+    return lax.dynamic_index_in_dim(value, index, axis, keepdims=False)
+
+
+def vmem_call(body, outs, scratch=(), flops=0, moved=0):
+    return pl.pallas_call(
+        body,
+        out_shape=outs,
+        scratch_shapes=list(scratch),
+        compiler_params=pltpu.CompilerParams(vmem_limit_bytes=40 * 2**20),
+        cost_estimate=pl.CostEstimate(flops=flops, bytes_accessed=moved, transcendentals=0),
+    )
+
+
+def place_blocks(place_ref, blocks_ref, out_ref):
+    rows = blocks_ref.shape[1]
+    for block in range(blocks_ref.shape[0]):
+        start = pl.multiple_of(place_ref[block] * rows, 16)
+        out_ref[pl.ds(start, rows), :] = blocks_ref[block]
+
+
+def gathered(value):
+    rows, lanes = value.shape
+    z, y, c = coordinates()
+    line = jnp.stack([value] + [shifted(value, dz=step) for step in range(1, GRID[0])])
+    plane = jnp.stack([line, shifted(line, dy=1)])
+    other = shifted(plane, dc=1)
+    pair = jnp.where(c == 0, jnp.stack([plane, other], 2), jnp.stack([other, plane], 2))
+    blocks = pair.reshape(GRID[0] * GRID[1], GRID[2] * rows, lanes)
+    places = jnp.stack(
+        [
+            ((z - step) % GRID[0]) * GRID[1] + (y + dy) % GRID[1]
+            for dy in range(GRID[1])
+            for step in range(GRID[0])
+        ]
+    ).astype(jnp.int32)
+    total = GRID[0] * GRID[1] * GRID[2] * rows
+    return pl.pallas_call(
+        place_blocks,
+        out_shape=jax.ShapeDtypeStruct((total, lanes), value.dtype),
+        in_specs=[
+            pl.BlockSpec(memory_space=pltpu.SMEM),
+            pl.BlockSpec(memory_space=pltpu.VMEM),
+        ],
+        compiler_params=pltpu.CompilerParams(vmem_limit_bytes=40 * 2**20),
+        cost_estimate=pl.CostEstimate(
+            flops=0, bytes_accessed=4 * total * lanes, transcendentals=0
+        ),
+    )(places, blocks)
+
+
+def added(*terms):
+    return sum(term.astype(F32) for term in terms)
+
+
+def summed_on_chip(value):
+    _, _, c = coordinates()
+    sent = shifted(part_of(value, 1 - c, 2), dc=1)
+    return added(part_of(value, c, 2), sent).astype(BF16)
+
+
+def summed_over_chips(value):
+    z, y, _ = coordinates()
+    sent = shifted(part_of(value, 1 - y, 1), dy=1)
+    line = added(part_of(value, y, 1), sent).astype(BF16)
+    terms = [part_of(line, z, 0)] + [
+        shifted(part_of(line, (z + step) % GRID[0], 0), dz=step) for step in range(1, GRID[0])
+    ]
+    return added(*terms)
+
+
+def scattered(value):
+    lanes = value.shape[1]
+    return summed_over_chips(summed_on_chip(value.reshape(*GRID, -1, lanes)))
+
+
+def pixel_masks(rows):
+    row = lax.broadcasted_iota(jnp.int32, (rows, 1), 0)
+    high, wide = (row // WIDTH) % HEIGHT, row % WIDTH
+    masks = []
+    for dr in (-1, 0, 1):
+        for dc in (-1, 0, 1):
+            inside = (high + dr >= 0) & (high + dr < HEIGHT) & (wide + dc >= 0) & (wide + dc < WIDTH)
+            masks.append((dr * WIDTH + dc, inside))
+    return masks
+
+
+def frame_masks(rows, frames):
+    pixels = HEIGHT * WIDTH
+    row = lax.broadcasted_iota(jnp.int32, (rows, 1), 0)
+    frame = (row // pixels) % frames
+    return [
+        (step * pixels, (frame + step >= 0) & (frame + step < frames)) for step in (-1, 0, 1)
+    ]
+
+
+def moved_rows(value, move):
+    shift, inside = move
+    if shift:
+        value = pltpu.roll(value, (-shift) % value.shape[0], 0)
+    return jnp.where(inside, value, 0.0)
+
+
+def dot(left, right, dims=((1,), (0,))):
+    return lax.dot_general(left, right, (dims, ((), ())), preferred_element_type=F32)
+
+
+def with_embedding(hidden, embedding_ref, samples):
+    per = hidden.shape[0] // samples
+    return jnp.concatenate(
+        [hidden[s * per : (s + 1) * per] + embedding_ref[s : s + 1, :] for s in range(samples)]
+    )
+
+
+def scale_of(summed):
+    return lax.rsqrt(jnp.mean(summed * summed, axis=-1, keepdims=True) + 1e-06)
+
+
+def silu_parts(preact):
+    logistic = 1.0 / (1.0 + jnp.exp(-preact))
+    return logistic, preact * logistic
+
+
+def convolved(normed, weight_ref, masks):
+    rows, channels = normed.shape
+    normed = normed.astype(F32)
+    total = None
+    for tap in range(9):
+        term = dot(
+            moved_rows(normed, masks[tap]).astype(BF16),
+            weight_ref[tap * channels : (tap + 1) * channels, :],
+        )
+        total = term if total is None else total + term
+    return total
+
+
+def first_forward(frames, hidden_ref, embedding_ref, keep_ref, spatial_ref, temporal_ref, *outs):
+    normed_ref, preact_ref, mixed_ref = outs
+    rows = hidden_ref.shape[0]
+    width = keep_ref.shape[1]
+    summed = with_embedding(hidden_ref[...].astype(F32), embedding_ref, embedding_ref.shape[0])
+    normed = (summed * scale_of(summed)).astype(BF16)
+    normed_ref[...] = normed
+    preact = convolved(normed, spatial_ref, pixel_masks(rows))
+    preact_ref[...] = preact
+    activated = silu_parts(preact)[1].astype(BF16).astype(F32) * keep_ref[...]
+    mixed = None
+    for tap, move in enumerate(frame_masks(rows, frames)):
+        term = dot(
+            moved_rows(activated, move).astype(BF16),
+            temporal_ref[tap * width : (tap + 1) * width, :],
+        )
+        mixed = term if mixed is None else mixed + term
+    mixed_ref[...] = mixed.astype(BF16)
+
+
+def slope_of(preact):
+    logistic, _ = silu_parts(preact)
+    return logistic * (1.0 + preact * (1.0 - logistic))
+
+
+def act_grad_of(upstream, temporal_ref, width, frames):
+    upstream = upstream.astype(F32)
+    moves = frame_masks(upstream.shape[0], frames)
+    total = None
+    for tap in range(3):
+        term = dot(
+            moved_rows(upstream, moves[2 - tap]).astype(BF16),
+            temporal_ref[tap * width : (tap + 1) * width, :],
+            ((1,), (1,)),
+        )
+        total = term if total is None else total + term
+    return total
+
+
+def store_temporal_terms(activated, upstream, frames, out_ref):
+    width = activated.shape[1]
+    upstream = upstream.astype(F32)
+    moves = frame_masks(upstream.shape[0], frames)
+    for tap in range(3):
+        out_ref[tap * width : (tap + 1) * width, :] = dot(
+            activated, moved_rows(upstream, moves[2 - tap]).astype(BF16), ((0,), (0,))
+        ).astype(BF16)
+
+
+def store_spatial_terms(normed, pre_grad, out_ref):
+    channels = normed.shape[1]
+    pre_grad = pre_grad.astype(F32)
+    masks = pixel_masks(pre_grad.shape[0])
+    for tap in range(9):
+        out_ref[tap * channels : (tap + 1) * channels, :] = dot(
+            normed, moved_rows(pre_grad, masks[8 - tap]).astype(BF16), ((0,), (0,))
+        ).astype(BF16)
+
+
+def second_forward(
+    frames, hidden_ref, own_ref, sent_ref, embedding_ref, keep_ref, upstream_ref, spatial_ref,
+    temporal_ref, next_ref, normed_ref, activated_ref, pre_grad_ref, back_ref,
+):
+    rows, channels = hidden_ref.shape
+    width = keep_ref.shape[1]
+    masks = pixel_masks(rows)
+    mixed = own_ref[...].astype(F32) + sent_ref[...].astype(F32)
+    hidden = (hidden_ref[...].astype(F32) + mixed).astype(BF16)
+    next_ref[...] = hidden
+    summed = with_embedding(hidden.astype(F32), embedding_ref, embedding_ref.shape[0])
+    normed = (summed * scale_of(summed)).astype(BF16)
+    normed_ref[...] = normed
+    preact = convolved(normed, spatial_ref, masks)
+    activated_ref[...] = (silu_parts(preact)[1] * keep_ref[...]).astype(BF16)
+    act_grad = act_grad_of(upstream_ref[...], temporal_ref, width, frames)
+    pre_grad = (act_grad * slope_of(preact) * keep_ref[...]).astype(BF16)
+    pre_grad_ref[...] = pre_grad
+    pre_grad = pre_grad.astype(F32)
+    back = None
+    for tap in range(9):
+        term = dot(
+            moved_rows(pre_grad, masks[8 - tap]).astype(BF16),
+            spatial_ref[tap * channels : (tap + 1) * channels, :],
+            ((1,), (1,)),
+        )
+        back = term if back is None else back + term
+    back_ref[...] = back.astype(BF16)
+
+
+def second_terms(frames, normed_ref, pre_grad_ref, activated_ref, upstream_ref, *outs):
+    spatial_ref, temporal_ref = outs
+    store_spatial_terms(normed_ref[...], pre_grad_ref[...], spatial_ref)
+    store_temporal_terms(activated_ref[...], upstream_ref[...], frames, temporal_ref)
+
+
+def first_terms(
+    frames, hidden_ref, embedding_ref, upstream_ref, own_ref, sent_ref, normed_ref, preact_ref,
+    keep_ref, temporal_ref, spatial_out, temporal_out,
+):
+    width = keep_ref.shape[1]
+    channels = hidden_ref.shape[1]
+    summed = with_embedding(hidden_ref[...].astype(F32), embedding_ref, embedding_ref.shape[0])
+    scale = scale_of(summed)
+    grad = own_ref[...].astype(F32) + sent_ref[...].astype(F32)
+    inner = jnp.sum(grad * summed, axis=-1, keepdims=True)
+    back = grad * scale - summed * (scale * scale * scale) * (inner / channels)
+    upstream = (upstream_ref[...].astype(F32) + back).astype(BF16)
+    preact = preact_ref[...]
+    activated = (silu_parts(preact)[1] * keep_ref[...]).astype(BF16)
+    act_grad = act_grad_of(upstream, temporal_ref, width, frames)
+    pre_grad = (act_grad * slope_of(preact) * keep_ref[...]).astype(BF16)
+    store_spatial_terms(normed_ref[...], pre_grad, spatial_out)
+    store_temporal_terms(activated, upstream, frames, temporal_out)
+
+
+def paired_device(samples, timesteps, cotangent, spatial_weight, temporal_weight):
+    me = lax.axis_index("pipe")
+    first = me == 0
+    _, _, c = coordinates()
+    count, frames, pixels, channels = samples.shape
+    rows = count * frames * pixels
+    main = 2 * LANES
+    width = main + LANES
+    hidden = samples.reshape(rows, channels)
+    upstream = cotangent.reshape(rows, channels)
+    embedding = jax.vmap(lambda step: embedding_of(step, channels))(timesteps)
+    lane = jnp.arange(LANES)
+    keep_own = jnp.concatenate([jnp.ones(main), lane < LANES // 2]).astype(F32)[None]
+    keep_other = jnp.concatenate([jnp.ones(main), lane >= LANES // 2]).astype(F32)[None]
+    keep_first = jnp.where(first, keep_own, keep_other)
+    keep_second = jnp.where(first, keep_other, keep_own)
+    tail = lane[None] < LANES // 2
+
+    def main_of(value, index, axis):
+        return lax.dynamic_slice_in_dim(value, index * main, main, axis)
+
+    temporal_own = gathered(temporal_weight[0]).reshape(3, channels, channels)
+    spatial_own = spatial_weight[0]
+    given = swapped(
+        jnp.concatenate([main_of(spatial_own, 1 - me, 1), spatial_own[:, 2 * main :]], 1)
+    )
+    main_own, main_given = main_of(spatial_own, me, 1), given[:, :main]
+    tails = jnp.where(tail, spatial_own[:, 2 * main :], given[:, main:])
+    spatial_first = gathered(jnp.concatenate([jnp.where(first, main_own, main_given), tails], 1))
+    main_second = gathered(jnp.where(first, main_given, main_own))
+    spatial_second = jnp.concatenate([main_second, spatial_first[:, main:]], 1)
+
+    def local_rows(index):
+        return jnp.concatenate(
+            [main_of(temporal_own, index, 1), temporal_own[:, 2 * main :]], 1
+        ).reshape(GRID[2], -1, channels)
+
+    half = swapped(part_of(local_rows(1 - me), c, 0))
+    other_half = shifted(half, dc=1)
+    temporal_other = jnp.where(
+        c == 0, jnp.concatenate([half, other_half]), jnp.concatenate([other_half, half])
+    )
+    temporal_mine = local_rows(me).reshape(3 * width, channels)
+    temporal_first = jnp.where(first, temporal_mine, temporal_other)
+    temporal_second = jnp.where(first, temporal_other, temporal_mine)
+
+    def shape(extent, dtype=BF16):
+        return jax.ShapeDtypeStruct(extent, dtype)
+
+    spatial_flops = 2 * rows * 9 * channels * width
+    temporal_flops = 2 * rows * 3 * channels * width
+    spatial_bytes = 2 * 9 * channels * width
+    temporal_bytes = 2 * 3 * channels * width
+    normed_first, preact_first, mixed = vmem_call(
+        functools.partial(first_forward, frames),
+        (shape((rows, channels)), shape((rows, width), F32), shape((rows, channels))),
+        flops=spatial_flops + temporal_flops,
+        moved=spatial_bytes + temporal_bytes,
+    )(hidden, embedding, keep_first, spatial_first, temporal_first)
+    hidden_second, normed_second, activated_second, pre_grad_second, back = vmem_call(
+        functools.partial(second_forward, frames),
+        (
+            shape((rows, channels)),
+            shape((rows, channels)),
+            shape((rows, width)),
+            shape((rows, width)),
+            shape((rows, channels)),
+        ),
+        flops=2 * spatial_flops + temporal_flops,
+        moved=spatial_bytes + temporal_bytes,
+    )(
+        hidden, mixed, swapped(mixed), embedding, keep_second, upstream, spatial_second,
+        temporal_second,
+    )
+
+    back_given = swapped(back)
+    spatial_terms_second, temporal_terms_second = vmem_call(
+        functools.partial(second_terms, frames),
+        (shape((9 * channels, width)), shape((3 * width, channels))),
+        flops=spatial_flops + temporal_flops,
+        moved=spatial_bytes + temporal_bytes,
+    )(normed_second, pre_grad_second, activated_second, upstream)
+    grad_second = scattered(spatial_terms_second[:, :main])
+    spatial_terms_first, temporal_terms_first = vmem_call(
+        functools.partial(first_terms, frames),
+        (shape((9 * channels, width)), shape((3 * width, channels))),
+        flops=spatial_flops + 2 * temporal_flops,
+        moved=spatial_bytes + 2 * temporal_bytes,
+    )(
+        hidden_second, embedding, upstream, back, back_given, normed_first, preact_first,
+        keep_first, temporal_first,
+    )
+    tail_terms = spatial_terms_first[:, main:] + spatial_terms_second[:, main:]
+    grad_first = scattered(jnp.concatenate([spatial_terms_first[:, :main], tail_terms], 1))
+
+    terms = jnp.stack(
+        [
+            jnp.where(first, temporal_terms_first, temporal_terms_second),
+            jnp.where(first, temporal_terms_second, temporal_terms_first),
+        ]
+    ).reshape(2, GRID[2], -1, channels)
+    sent = shifted(part_of(terms, 1 - c, 1), dc=1)
+    halves = added(part_of(terms, c, 1), sent).astype(BF16)
+    halves = jnp.stack([halves[0], swapped(halves[1])])
+    other_halves = shifted(halves, dc=1)
+    both = jnp.where(
+        c == 0,
+        jnp.stack([halves, other_halves], 1),
+        jnp.stack([other_halves, halves], 1),
+    ).reshape(2, 3, width, channels)
+    mine, theirs = both[0], both[1]
+    full = jnp.concatenate(
+        [
+            jnp.where(first, mine[:, :main], theirs[:, :main]),
+            jnp.where(first, theirs[:, :main], mine[:, :main]),
+            mine[:, main:] + theirs[:, main:],
+        ],
+        1,
+    )
+    share_temporal = summed_over_chips(part_of(full.reshape(*GRID, -1, channels), c, 2))
+
+    kept = jnp.where(first, grad_first[:, :main], grad_second)
+    passed = jnp.where(first, grad_second, grad_first[:, :main])
+    given = swapped(jnp.concatenate([passed, grad_first[:, main:]], 1).astype(BF16)).astype(F32)
+    share_spatial = jnp.concatenate(
+        [
+            jnp.where(first, kept, given[:, :main]),
+            jnp.where(first, given[:, :main], kept),
+            jnp.where(tail, grad_first[:, main:], given[:, main:]),
+        ],
+        1,
+    )
+    return (share_spatial[None], share_temporal[None])
+
+
 def solution(mesh):
+    paired = mesh.shape["pipe"] == 2 and mesh.shape["dp"] == math.prod(GRID)
     return jax.shard_map(
-        per_device,
+        paired_device if paired else per_device,
         mesh=mesh,
         in_specs=(
             P("dp", None, None, None),

time: 994 us -> 309 us (0.31)
  waiting for transfers between devices: 400 us -> 132 us
  local copies, waits for them, and re-layouts: 271 us -> 19.6 us
  matrix products: 180 us -> 0 us
  starting transfers between devices: 18.7 us -> 84.6 us
  other arithmetic: 87.9 us -> 36 us
  Pallas kernels: 0 us -> 28.5 us
  loops' own time: 18.3 us -> 0 us
  between operations: 13.8 us -> 1.64 us
    dot_general x35 -> x0, matrix products: 180 us -> none  [the longest x5 62.6 us: backward_second(): jnp.dot(columns.T, pre_grad, preferred_element_type=jnp.float32)]
    unnamed x6 -> x0, waiting for transfers between devices: 147 us -> none
    all_gather x2 -> x0, waiting for transfers between devices: 116 us -> none  [the longest x1 69.5 us: per_device(): lax.all_gather(spatial_weight[0], 'dp', axis=0, tiled=True)]
    ppermute x12 -> x38, starting transfers between devices: 18.5 us -> 84.6 us  [the longest x32 75.3 us: shifted(): return lax.ppermute(value, 'dp', pairs)]
    slice x30 -> x8, local copies, waits for them, and re-layouts: 64.5 us -> 1.82 us  [the longest x1 0.9 us: paired_device(): spatial_own[:, 2 * main:]]
    concatenate x90 -> x0, local copies, waits for them, and re-layouts: 61.9 us -> none  [spatial_columns(): jnp.concatenate(pieces, axis=-1).reshape(frames * pixels, 9 * channels)]
    scatter-add x40 -> x0, local copies, waits for them, and re-layouts: 58.4 us -> none  [the longest x35 58.2 us: spatial_fold(): padded.at[:, row:row + HEIGHT, col:col + WIDTH, :]]
    pallas_call x0 -> x7, Pallas kernels: none -> 28.5 us  [the longest x1 8.8 us: paired_device(): vmem_call(functools.partial(second_forward, frames), (shape((rows, channe...]
  transfers between devices with their start and end apart: 16 -> 38, of which waited for: 16 -> 18; matrix products, arithmetic and copies ran while one was open for 1% -> 11% of each run, Pallas kernels for 0% -> 2%
where the time goes in v1:
time: 309 us; the launch traced here: 303 us
  waiting for transfers between devices  132 us (43%)
  starting transfers between devices  84.6 us (27%)
  other arithmetic  36 us (12%)
  Pallas kernels  28.5 us (9%)
  local copies, waits for them, and re-layouts  19.6 us (6%)
    ppermute x32, waiting for transfers between devices, shifted(): return lax.ppermute(value, 'dp', pairs)  77.7 us
    ppermute x32, starting transfers between devices, shifted(): return lax.ppermute(value, 'dp', pairs)  75.3 us
    ppermute x6, waiting for transfers between devices, swapped(): return lax.ppermute(value, 'pipe', [(0, 1), (1, 0)])  54.7 us
    ppermute x6, starting transfers between devices, swapped(): return lax.ppermute(value, 'pipe', [(0, 1), (1, 0)])  9.22 us
    pallas_call x1, Pallas kernels, paired_device(): vmem_call(functools.partial(second_forward, frames), (shape((rows, channe...  8.8 us
    unnamed x44, local copies, waits for them, and re-layouts  7.37 us
    pallas_call x1, Pallas kernels, paired_device(): vmem_call(functools.partial(first_terms, frames), (shape((9 * channels, w...  6.63 us
    pallas_call x1, Pallas kernels, paired_device(): vmem_call(functools.partial(first_forward, frames), (shape((rows, channel...  6.26 us
  transfers between devices with their start and end apart: 38, of which 18 were waited for; matrix products, arithmetic and copies ran while one was open for 11% of the time, Pallas kernels for 2%

profile of v1, /device:TPU:0, one launch (start us, length us, event | category | flops | bytes accessed | tf_op | source)
XLA Modules:
  0.0 302.6 jit_solution(15410530544968589051)
XLA Ops:
  0.6 3.1 %collective-permute-start.6 = (bf16[120,640]{1,0:T(8,128)(2,1)}, bf16[120,640]{1,0:T(8,128)(2,1)S(1)}, u32[]{:S(2)}, u32[]{:S(2)}) collective-permute-start(bf16[120,640]{1,0:T(8,128)(2,1)} %bitcast.175), channel_id=1, source_target_pairs={{0,4},{1,5},{2,6},{3,7},{4,8},{5,9},{6,10},{7,11},{8,12},{9,13},{1... | collective-permute-start | bytes 460808 | tf_op jit(solution)/shard_map/ppermute | solution.py:233
  3.7 2.6 collective-permute-start.7
  6.3 1.3 collective-permute-start.8
  9.6 1.6 collective-permute-start
  11.2 5.4 %collective-permute-done.7 = bf16[120,640]{1,0:T(8,128)(2,1)S(1)} collective-permute-done((bf16[120,640]{1,0:T(8,128)(2,1)}, bf16[120,640]{1,0:T(8,128)(2,1)S(1)}, u32[]{:S(2)}, u32[]{:S(2)}) %collective-permute-start.7) | collective-permute-done | bytes 153632 | tf_op jit(solution)/shard_map/ppermute | solution.py:233
  17.6 1.6 collective-permute-start.9
  19.4 3.8 %collective-permute-start.1 = (bf16[360,384]{1,0:T(8,128)(2,1)S(1)}, bf16[360,384]{1,0:T(8,128)(2,1)S(1)}, u32[]{:S(2)}, u32[]{:S(2)}) collective-permute-start(bf16[360,384]{1,0:T(8,128)(2,1)S(1)} %get-tuple-element.74), channel_id=1, source_target_pairs={{0,4},{1,5},{2,6},{3,7},{4,8},{5,9},{6,10},{7,11},{8,12},{9,13},{1... | collective-permute-start | bytes 829448 | tf_op jit(solution)/shard_map/ppermute | solution.py:233
  23.2 1.6 collective-permute-start.2
  25.7 1.2 collective-permute-start.14
  26.9 5.1 %collective-permute-done.1 = bf16[360,384]{1,0:T(8,128)(2,1)S(1)} collective-permute-done((bf16[360,384]{1,0:T(8,128)(2,1)S(1)}, bf16[360,384]{1,0:T(8,128)(2,1)S(1)}, u32[]{:S(2)}, u32[]{:S(2)}) %collective-permute-start.1) | collective-permute-done | bytes 276512 | tf_op jit(solution)/shard_map/ppermute | solution.py:233
  32.0 1.2 collective-permute-start.15
  33.2 10.7 %collective-permute-done.2 = bf16[360,384]{1,0:T(8,128)(2,1)S(1)} collective-permute-done((bf16[360,384]{1,0:T(8,128)(2,1)S(1)}, bf16[360,384]{1,0:T(8,128)(2,1)S(1)}, u32[]{:S(2)}, u32[]{:S(2)}) %collective-permute-start.2) | collective-permute-done | bytes 276512 | tf_op jit(solution)/shard_map/ppermute | solution.py:233
  43.8 12.9 %collective-permute-start.16 = (bf16[360,256]{1,0:T(8,128)(2,1)S(1)}, bf16[360,256]{1,0:T(8,128)(2,1)S(1)}, u32[]{:S(2)}, u32[]{:S(2)}) collective-permute-start(bf16[360,256]{1,0:T(8,128)(2,1)S(1)} %get-tuple-element.64), channel_id=1, source_target_pairs={{0,12},{1,13},{2,14},{3,15},{4,0},{5,1},{6,2},{7,3},{8,4},{9,5},{1... | collective-permute-start | bytes 552968 | tf_op jit(solution)/shard_map/ppermute | solution.py:233
  56.8 1.6 fusion.24
  58.9 1.2 fusion.18
  60.2 1.6 collective-permute-start.17
  61.9 31.9 %collective-permute-done.17 = bf16[4,360,256]{2,1,0:T(8,128)(2,1)} collective-permute-done((bf16[4,360,256]{2,1,0:T(8,128)(2,1)S(1)}, bf16[4,360,256]{2,1,0:T(8,128)(2,1)}, u32[]{:S(2)}, u32[]{:S(2)}) %collective-permute-start.17) | collective-permute-done | bytes 737312 | tf_op jit(solution)/shard_map/ppermute | solution.py:233
  93.8 1.4 fusion.21
  95.4 1.6 fusion.23
  97.5 2.3 maximum_select_fusion.3
  101.4 1.6 collective-permute-start.11
  103.0 16.9 %collective-permute-done.11 = bf16[576,640]{1,0:T(8,128)(2,1)S(1)} collective-permute-done((bf16[576,640]{1,0:T(8,128)(2,1)S(1)}, bf16[576,640]{1,0:T(8,128)(2,1)S(1)}, u32[]{:S(2)}, u32[]{:S(2)}) %collective-permute-start.11) | collective-permute-done | bytes 737312 | tf_op jit(solution)/shard_map/ppermute | solution.py:237
  122.9 3.3 %maximum_select_fusion = bf16[2,4,2,360,384]{4,3,1,0,2:T(8,128)(2,1)S(1)} fusion(bf16[2,4,1,360,384]{4,3,1,0,2:T(8,128)(2,1)} %bitcast.19, bf16[2,4,1,360,384]{4,3,1,0,2:T(8,128)(2,1)S(1)} %get-tuple-element.42, pred[]{:T(512)S(6)} %eq.81), kind=kLoop, calls=%fused_computation | loop fusion | flops 6635520 | bytes 8847361 | tf_op jit(solution)/shard_map/jit(_where)/select_n | solution.py:267
  128.7 6.3 %shard_map.70 = (bf16[480,640]{1,0:T(8,128)(2,1)S(1)}, f32[480,384]{1,0:T(8,128)S(1)}, bf16[480,640]{1,0:T(8,128)(2,1)S(1)}) custom-call(bf16[480,640]{1,0:T(8,128)(2,1)S(1)} %bitcast.145, f32[5,640]{1,0:T(8,128)S(1)} %pad_maximum_fusion.15.embedding_ref, f32[1,384]{1,0:T(1,128)S(1)} %select_n.386.keep_ref, bf16[5760,384]{1,0:T(8,128)(2,1)S(1)} %shard_map.68.spatial_ref, ...), custom_call_target="tpu_custom_call" | custom-call | flops 2831155200 | bytes 5898240 | tf_op jit(solution)/shard_map/pallas_call | solution.py:544
  135.0 1.6 collective-permute-start.13
  137.1 13.9 %collective-permute-done.13.sent_ref = bf16[480,640]{1,0:T(8,128)(2,1)S(1)} collective-permute-done((bf16[480,640]{1,0:T(8,128)(2,1)S(1)}, bf16[480,640]{1,0:T(8,128)(2,1)S(1)}, u32[]{:S(2)}, u32[]{:S(2)}) %collective-permute-start.13) | collective-permute-done | bytes 614432 | tf_op jit(solution)/shard_map/ppermute | solution.py:237
  151.0 8.8 %shard_map.72 = (bf16[480,640]{1,0:T(8,128)(2,1)S(1)}, bf16[480,640]{1,0:T(8,128)(2,1)S(1)}, bf16[480,384]{1,0:T(8,128)(2,1)S(1)}, bf16[480,384]{1,0:T(8,128)(2,1)S(1)}, bf16[480,640]{1,0:T(8,128)(2,1)S(1)}) custom-call(bf16[480,640]{1,0:T(8,128)(2,1)S(1)} %bitcast.146, bf16[480,640]{1,0:T(8,128)(2,1)S(1)} %get-tuple-element.14.own_ref, ...), custom_call_target="tpu_custom_call" | custom-call | flops 4954521600 | bytes 5898240 | tf_op jit(solution)/shard_map/pallas_call | solution.py:550
  163.0 1.5 collective-permute-start.19
  164.5 1.1 copy-done.9
  167.5 4.4 %shard_map.74 = (bf16[5760,384]{1,0:T(8,128)(2,1)S(1)}, bf16[1152,640]{1,0:T(8,128)(2,1)S(1)}) custom-call(bf16[480,640]{1,0:T(8,128)(2,1)S(1)} %copy-done.9, bf16[480,384]{1,0:T(8,128)(2,1)S(1)} %copy-done.13, bf16[480,384]{1,0:T(8,128)(2,1)S(1)} %copy-done.11, bf16[480,640]{1,0:T(8,128)(2,1)S(1)} %bitcast.148), custom_call_target="tpu_custom_call" | custom-call | flops 2831155200 | bytes 5898240 | tf_op jit(solution)/shard_map/pallas_call | solution.py:567
  171.9 6.2 %collective-permute-done.19.sent_ref = bf16[480,640]{1,0:T(8,128)(2,1)S(1)} collective-permute-done((bf16[480,640]{1,0:T(8,128)(2,1)S(1)}, bf16[480,640]{1,0:T(8,128)(2,1)S(1)}, u32[]{:S(2)}, u32[]{:S(2)}) %collective-permute-start.19) | collective-permute-done | bytes 614432 | tf_op jit(solution)/shard_map/ppermute | solution.py:237
  178.0 6.6 %shard_map.73 = (bf16[5760,384]{1,0:T(8,128)(2,1)S(1)}, bf16[1152,640]{1,0:T(8,128)(2,1)S(1)}) custom-call(bf16[480,640]{1,0:T(8,128)(2,1)S(1)} %copy-done.7, f32[5,640]{1,0:T(8,128)S(1)} %pad_maximum_fusion.15.embedding_ref, bf16[480,640]{1,0:T(8,128)(2,1)S(1)} %bitcast.149, bf16[480,640]{1,0:T(8,128)(2,1)S(1)} %get-tuple-element.16.own_ref, ...), custom_call_target="tpu_custom_call" | custom-call | flops 3538944000 | bytes 7372800 | tf_op jit(solution)/shard_map/pallas_call | solution.py:574
  185.5 1.8 constant_dynamic-slice_fusion.3
  187.3 1.6 copy.31
  189.2 1.4 fusion.5
  191.3 1.4 constant_dynamic-slice_fusion.1
  192.7 1.2 copy.32
  193.9 1.8 collective-permute-done.31
  195.7 1.9 fusion.1
  197.8 2.2 fusion
  200.8 1.6 collective-permute-start.32
  202.3 1.8 fusion.2
  205.1 1.5 collective-permute-start.26
  206.7 12.4 %collective-permute-done.32 = bf16[576,640]{1,0:T(8,128)(2,1)S(1)} collective-permute-done((bf16[576,640]{1,0:T(8,128)(2,1)S(1)}, bf16[576,640]{1,0:T(8,128)(2,1)S(1)}, u32[]{:S(2)}, u32[]{:S(2)}) %collective-permute-start.32) | collective-permute-done | bytes 737312 | tf_op jit(solution)/shard_map/ppermute | solution.py:237
  219.1 1.9 fusion.20
  221.0 6.5 %collective-permute-done.21 = bf16[4,360,384]{2,1,0:T(8,128)(2,1)} collective-permute-done((bf16[4,360,384]{2,1,0:T(8,128)(2,1)S(1)}, bf16[4,360,384]{2,1,0:T(8,128)(2,1)}, u32[]{:S(2)}, u32[]{:S(2)}) %collective-permute-start.21) | collective-permute-done | bytes 1105952 | tf_op jit(solution)/shard_map/ppermute | solution.py:233
  227.5 1.5 fusion.3
  229.1 6.3 %collective-permute-start.22 = (bf16[360,384]{1,0:T(8,128)(2,1)S(1)}, bf16[360,384]{1,0:T(8,128)(2,1)S(1)}, u32[]{:S(2)}, u32[]{:S(2)}) collective-permute-start(bf16[360,384]{1,0:T(8,128)(2,1)S(1)} %get-tuple-element.54), channel_id=1, source_target_pairs={{0,4},{1,5},{2,6},{3,7},{4,8},{5,9},{6,10},{7,11},{8,12},{9,13},{1... | collective-permute-start | bytes 829448 | tf_op jit(solution)/shard_map/ppermute | solution.py:233
  235.4 2.4 collective-permute-start.24
  237.9 4.6 %collective-permute-done.26 = bf16[4,360,256]{2,1,0:T(8,128)(2,1)} collective-permute-done((bf16[4,360,256]{2,1,0:T(8,128)(2,1)}, bf16[4,360,256]{2,1,0:T(8,128)(2,1)}, u32[]{:S(2)}, u32[]{:S(2)}) %collective-permute-start.26) | collective-permute-done | bytes 737312 | tf_op jit(solution)/shard_map/ppermute | solution.py:233
  242.5 1.3 fusion.8
  243.8 6.3 %collective-permute-start.27 = (bf16[360,256]{1,0:T(8,128)(2,1)S(1)}, bf16[360,256]{1,0:T(8,128)(2,1)S(1)}, u32[]{:S(2)}, u32[]{:S(2)}) collective-permute-start(bf16[360,256]{1,0:T(8,128)(2,1)S(1)} %get-tuple-element.59), channel_id=1, source_target_pairs={{0,4},{1,5},{2,6},{3,7},{4,8},{5,9},{6,10},{7,11},{8,12},{9,13},{1... | collective-permute-start | bytes 552968 | tf_op jit(solution)/shard_map/ppermute | solution.py:233
  250.1 5.0 %collective-permute-start.28 = (bf16[360,256]{1,0:T(8,128)(2,1)S(1)}, bf16[360,256]{1,0:T(8,128)(2,1)S(1)}, u32[]{:S(2)}, u32[]{:S(2)}) collective-permute-start(bf16[360,256]{1,0:T(8,128)(2,1)S(1)} %get-tuple-element.61), channel_id=1, source_target_pairs={{0,8},{1,9},{2,10},{3,11},{4,12},{5,13},{6,14},{7,15},{8,0},{9,1},... | collective-permute-start | bytes 552968 | tf_op jit(solution)/shard_map/ppermute | solution.py:233
  255.1 13.9 %collective-permute-start.29 = (bf16[360,256]{1,0:T(8,128)(2,1)S(1)}, bf16[360,256]{1,0:T(8,128)(2,1)S(1)}, u32[]{:S(2)}, u32[]{:S(2)}) collective-permute-start(bf16[360,256]{1,0:T(8,128)(2,1)S(1)} %get-tuple-element.60), channel_id=1, source_target_pairs={{0,12},{1,13},{2,14},{3,15},{4,0},{5,1},{6,2},{7,3},{8,4},{9,5},{1... | collective-permute-start | bytes 552968 | tf_op jit(solution)/shard_map/ppermute | solution.py:233
  269.2 2.9 collective-permute-done.29
  272.3 2.4 maximum_select_fusion.2
  277.6 1.5 collective-permute-start.30
  279.1 5.3 %collective-permute-done.30 = bf16[360,384]{1,0:T(8,128)(2,1)} collective-permute-done((bf16[360,384]{1,0:T(8,128)(2,1)}, bf16[360,384]{1,0:T(8,128)(2,1)}, u32[]{:S(2)}, u32[]{:S(2)}) %collective-permute-start.30) | collective-permute-done | bytes 276512 | tf_op jit(solution)/shard_map/ppermute | solution.py:237
  285.5 2.4 collective-permute-done.34
  287.9 1.2 fusion.9
  289.2 3.0 collective-permute-start.35
  292.2 2.3 collective-permute-start.36
  295.7 1.6 collective-permute-done.35
  297.2 3.9 %collective-permute-done.36 = bf16[120,640]{1,0:T(8,128)(2,1)S(1)} collective-permute-done((bf16[120,640]{1,0:T(8,128)(2,1)S(1)}, bf16[120,640]{1,0:T(8,128)(2,1)S(1)}, u32[]{:S(2)}, u32[]{:S(2)}) %collective-permute-start.36) | collective-permute-done | bytes 153632 | tf_op jit(solution)/shard_map/ppermute | solution.py:233
  (136 shorter events, 28.3 us)
Async XLA Ops:
  0.6 10.5 %collective-permute-start.6 = (bf16[120,640]{1,0:T(8,128)(2,1)}, bf16[120,640]{1,0:T(8,128)(2,1)S(1)}, u32[]{:S(2)}, u32[]{:S(2)}) collective-permute-start(bf16[120,640]{1,0:T(8,128)(2,1)} %bitcast.175), channel_id=1, source_target_pairs={{0,4},{1,5},{2,6},{3,7},{4,8},{5,9},{6,10},{7,11},{8,12},{9,13},{1... | collective-permute-start | bytes 460808 | tf_op jit(solution)/shard_map/ppermute | solution.py:233
  3.7 12.9 %collective-permute-start.7 = (bf16[120,640]{1,0:T(8,128)(2,1)}, bf16[120,640]{1,0:T(8,128)(2,1)S(1)}, u32[]{:S(2)}, u32[]{:S(2)}) collective-permute-start(bf16[120,640]{1,0:T(8,128)(2,1)} %bitcast.176), channel_id=1, source_target_pairs={{0,8},{1,9},{2,10},{3,11},{4,12},{5,13},{6,14},{7,15},{8,0},{9,1},... | collective-permute-start | bytes 460808 | tf_op jit(solution)/shard_map/ppermute | solution.py:233
  6.3 10.3 %collective-permute-start.8 = (bf16[120,640]{1,0:T(8,128)(2,1)}, bf16[120,640]{1,0:T(8,128)(2,1)S(1)}, u32[]{:S(2)}, u32[]{:S(2)}) collective-permute-start(bf16[120,640]{1,0:T(8,128)(2,1)} %bitcast.177), channel_id=1, source_target_pairs={{0,12},{1,13},{2,14},{3,15},{4,0},{5,1},{6,2},{7,3},{8,4},{9,5},{1... | collective-permute-start | bytes 460808 | tf_op jit(solution)/shard_map/ppermute | solution.py:233
  7.6 11.6 %copy-start.20 = (bf16[1,360,640]{2,1,0:T(8,128)(2,1)S(1)}, bf16[1,360,640]{2,1,0:T(8,128)(2,1)}, u32[]{:S(2)}) copy-start(bf16[1,360,640]{2,1,0:T(8,128)(2,1)} %param.8) | copy-start | bytes 1382404
  9.6 9.6 %collective-permute-start = (bf16[360,384]{1,0:T(8,128)(2,1)S(1)}, bf16[360,384]{1,0:T(8,128)(2,1)S(1)}, u32[]{:S(2)}, u32[]{:S(2)}) collective-permute-start(bf16[360,384]{1,0:T(8,128)(2,1)S(1)} %pad_maximum_fusion.12), channel_id=1, source_target_pairs={{0,16},{16,0},{1,17},{17,1},{2,18},{18,2},{3,19},{19,3},{4,20},{20... | collective-permute-start | bytes 829448 | tf_op jit(solution)/shard_map/ppermute | solution.py:237
  17.6 41.2 %collective-permute-start.9 = (bf16[4,120,640]{2,1,0:T(8,128)(2,1)S(1)}, bf16[4,120,640]{2,1,0:T(8,128)(2,1)S(1)}, u32[]{:S(2)}, u32[]{:S(2)}) collective-permute-start(bf16[4,120,640]{2,1,0:T(8,128)(2,1)S(1)} %get-tuple-element.70), channel_id=1, source_target_pairs={{0,2},{1,3},{2,0},{3,1},{4,6},{5,7},{6,4},{7,5},{8,10},{9,11},{10,... | collective-permute-start | bytes 1843208 | tf_op jit(solution)/shard_map/ppermute | solution.py:233
  19.4 12.5 %collective-permute-start.1 = (bf16[360,384]{1,0:T(8,128)(2,1)S(1)}, bf16[360,384]{1,0:T(8,128)(2,1)S(1)}, u32[]{:S(2)}, u32[]{:S(2)}) collective-permute-start(bf16[360,384]{1,0:T(8,128)(2,1)S(1)} %get-tuple-element.74), channel_id=1, source_target_pairs={{0,4},{1,5},{2,6},{3,7},{4,8},{5,9},{6,10},{7,11},{8,12},{9,13},{1... | collective-permute-start | bytes 829448 | tf_op jit(solution)/shard_map/ppermute | solution.py:233
  23.2 20.6 %collective-permute-start.2 = (bf16[360,384]{1,0:T(8,128)(2,1)S(1)}, bf16[360,384]{1,0:T(8,128)(2,1)S(1)}, u32[]{:S(2)}, u32[]{:S(2)}) collective-permute-start(bf16[360,384]{1,0:T(8,128)(2,1)S(1)} %get-tuple-element.74), channel_id=1, source_target_pairs={{0,8},{1,9},{2,10},{3,11},{4,12},{5,13},{6,14},{7,15},{8,0},{9,1},... | collective-permute-start | bytes 829448 | tf_op jit(solution)/shard_map/ppermute | solution.py:233
  24.9 31.9 %collective-permute-start.3 = (bf16[360,384]{1,0:T(8,128)(2,1)S(1)}, bf16[360,384]{1,0:T(8,128)(2,1)S(1)}, u32[]{:S(2)}, u32[]{:S(2)}) collective-permute-start(bf16[360,384]{1,0:T(8,128)(2,1)S(1)} %get-tuple-element.74), channel_id=1, source_target_pairs={{0,12},{1,13},{2,14},{3,15},{4,0},{5,1},{6,2},{7,3},{8,4},{9,5},{1... | collective-permute-start | bytes 829448 | tf_op jit(solution)/shard_map/ppermute | solution.py:233
  25.7 34.4 %collective-permute-start.14 = (bf16[360,256]{1,0:T(8,128)(2,1)S(1)}, bf16[360,256]{1,0:T(8,128)(2,1)S(1)}, u32[]{:S(2)}, u32[]{:S(2)}) collective-permute-start(bf16[360,256]{1,0:T(8,128)(2,1)S(1)} %get-tuple-element.64), channel_id=1, source_target_pairs={{0,4},{1,5},{2,6},{3,7},{4,8},{5,9},{6,10},{7,11},{8,12},{9,13},{1... | collective-permute-start | bytes 552968 | tf_op jit(solution)/shard_map/ppermute | solution.py:233
  32.0 28.1 %collective-permute-start.15 = (bf16[360,256]{1,0:T(8,128)(2,1)S(1)}, bf16[360,256]{1,0:T(8,128)(2,1)S(1)}, u32[]{:S(2)}, u32[]{:S(2)}) collective-permute-start(bf16[360,256]{1,0:T(8,128)(2,1)S(1)} %get-tuple-element.64), channel_id=1, source_target_pairs={{0,8},{1,9},{2,10},{3,11},{4,12},{5,13},{6,14},{7,15},{8,0},{9,1},... | collective-permute-start | bytes 552968 | tf_op jit(solution)/shard_map/ppermute | solution.py:233
  43.8 16.3 %collective-permute-start.16 = (bf16[360,256]{1,0:T(8,128)(2,1)S(1)}, bf16[360,256]{1,0:T(8,128)(2,1)S(1)}, u32[]{:S(2)}, u32[]{:S(2)}) collective-permute-start(bf16[360,256]{1,0:T(8,128)(2,1)S(1)} %get-tuple-element.64), channel_id=1, source_target_pairs={{0,12},{1,13},{2,14},{3,15},{4,0},{5,1},{6,2},{7,3},{8,4},{9,5},{1... | collective-permute-start | bytes 552968 | tf_op jit(solution)/shard_map/ppermute | solution.py:233
  58.3 37.0 %collective-permute-start.4 = (bf16[4,360,384]{2,1,0:T(8,128)(2,1)}, bf16[4,360,384]{2,1,0:T(8,128)(2,1)}, u32[]{:S(2)}, u32[]{:S(2)}) collective-permute-start(bf16[4,360,384]{2,1,0:T(8,128)(2,1)} %get-tuple-element.58), channel_id=1, source_target_pairs={{0,2},{1,3},{2,0},{3,1},{4,6},{5,7},{6,4},{7,5},{8,10},{9,11},{10,... | collective-permute-start | bytes 3317768 | tf_op jit(solution)/shard_map/ppermute | solution.py:233
  60.1 37.4 %collective-permute-start.10 = (bf16[2,4,120,640]{3,2,1,0:T(8,128)(2,1)}, bf16[2,4,120,640]{3,2,1,0:T(8,128)(2,1)}, u32[]{:S(2)}, u32[]{:S(2)}) collective-permute-start(bf16[2,4,120,640]{3,2,1,0:T(8,128)(2,1)} %get-tuple-element.53), channel_id=1, source_target_pairs={{0,1},{1,0},{2,3},{3,2},{4,5},{5,4},{6,7},{7,6},{8,9},{9,8},{10,11... | collective-permute-start | bytes 3686408 | tf_op jit(solution)/shard_map/ppermute | solution.py:233
  60.2 33.6 %collective-permute-start.17 = (bf16[4,360,256]{2,1,0:T(8,128)(2,1)S(1)}, bf16[4,360,256]{2,1,0:T(8,128)(2,1)}, u32[]{:S(2)}, u32[]{:S(2)}) collective-permute-start(bf16[4,360,256]{2,1,0:T(8,128)(2,1)S(1)} %get-tuple-element.63), channel_id=1, source_target_pairs={{0,2},{1,3},{2,0},{3,1},{4,6},{5,7},{6,4},{7,5},{8,10},{9,11},{10,... | collective-permute-start | bytes 2211848 | tf_op jit(solution)/shard_map/ppermute | solution.py:233
  93.8 1.5 copy-start.19
  95.3 24.8 %collective-permute-start.18 = (bf16[2,4,360,256]{3,2,1,0:T(8,128)(2,1)S(1)}, bf16[2,4,360,256]{3,2,1,0:T(8,128)(2,1)S(1)}, u32[]{:S(2)}, u32[]{:S(2)}) collective-permute-start(bf16[2,4,360,256]{3,2,1,0:T(8,128)(2,1)S(1)} %get-tuple-element.51), channel_id=1, source_target_pairs={{0,1},{1,0},{2,3},{3,2},{4,5},{5,4},{6,7},{7,6},{8,9},{9,8},{10,11... | collective-permute-start | bytes 4423688 | tf_op jit(solution)/shard_map/ppermute | solution.py:233
  97.0 25.9 %collective-permute-start.5 = (bf16[2,4,360,384]{3,2,1,0:T(8,128)(2,1)S(1)}, bf16[2,4,360,384]{3,2,1,0:T(8,128)(2,1)}, u32[]{:S(2)}, u32[]{:S(2)}) collective-permute-start(bf16[2,4,360,384]{3,2,1,0:T(8,128)(2,1)S(1)} %get-tuple-element.43), channel_id=1, source_target_pairs={{0,1},{1,0},{2,3},{3,2},{4,5},{5,4},{6,7},{7,6},{8,9},{9,8},{10,11... | collective-permute-start | bytes 6635528 | tf_op jit(solution)/shard_map/ppermute | solution.py:233
  101.3 1.7 copy-start.21
  101.4 18.5 %collective-permute-start.11 = (bf16[576,640]{1,0:T(8,128)(2,1)S(1)}, bf16[576,640]{1,0:T(8,128)(2,1)S(1)}, u32[]{:S(2)}, u32[]{:S(2)}) collective-permute-start(bf16[576,640]{1,0:T(8,128)(2,1)S(1)} %dynamic-slice_bitcast_fusion.2), channel_id=1, source_target_pairs={{0,16},{16,0},{1,17},{17,1},{2,18},{18,2},{3,19},{19,3},{4,20},{20... | collective-permute-start | bytes 2211848 | tf_op jit(solution)/shard_map/ppermute | solution.py:237
  119.9 2.2 collective-permute-start.12
  127.7 1.1 copy-start
  135.0 2.0 copy-start.2
  135.0 2.0 copy-start.4
  135.0 16.0 %copy-start.1 = (bf16[5,3,32,640]{3,2,1,0:T(8,128)(2,1)S(1)}, bf16[5,3,32,640]{3,2,1,0:T(8,128)(2,1)}, u32[]{:S(2)}) copy-start(bf16[5,3,32,640]{3,2,1,0:T(8,128)(2,1)} %param.7) | copy-start | bytes 1843204
  135.0 16.0 %collective-permute-start.13 = (bf16[480,640]{1,0:T(8,128)(2,1)S(1)}, bf16[480,640]{1,0:T(8,128)(2,1)S(1)}, u32[]{:S(2)}, u32[]{:S(2)}) collective-permute-start(bf16[480,640]{1,0:T(8,128)(2,1)S(1)} %get-tuple-element.14.own_ref), channel_id=1, source_target_pairs={{0,16},{16,0},{1,17},{17,1},{2,18},{18,2},{3,19},{19,3},{4,20},{20... | collective-permute-start | bytes 1843208 | tf_op jit(solution)/shard_map/ppermute | solution.py:237
  159.8 0.8 copy-start.6
  160.7 0.8 copy-start.8
  161.5 0.7 copy-start.10
  162.2 0.7 copy-start.12
  163.0 15.1 %collective-permute-start.19 = (bf16[480,640]{1,0:T(8,128)(2,1)S(1)}, bf16[480,640]{1,0:T(8,128)(2,1)S(1)}, u32[]{:S(2)}, u32[]{:S(2)}) collective-permute-start(bf16[480,640]{1,0:T(8,128)(2,1)S(1)} %get-tuple-element.16.own_ref), channel_id=1, source_target_pairs={{0,16},{16,0},{1,17},{17,1},{2,18},{18,2},{3,19},{19,3},{4,20},{20... | collective-permute-start | bytes 1843208 | tf_op jit(solution)/shard_map/ppermute | solution.py:237
  164.5 1.1 copy-start.9
  165.5 1.0 copy-start.11
  166.5 1.0 copy-start.13
  167.5 10.5 %copy-start.3 = (f32[480,384]{1,0:T(8,128)S(1)}, f32[480,384]{1,0:T(8,128)}, u32[]{:S(2)}) copy-start(f32[480,384]{1,0:T(8,128)} %copy-done.2) | copy-start | bytes 2211844
  167.5 10.5 %copy-start.5 = (bf16[480,640]{1,0:T(8,128)(2,1)S(1)}, bf16[480,640]{1,0:T(8,128)(2,1)}, u32[]{:S(2)}) copy-start(bf16[480,640]{1,0:T(8,128)(2,1)} %copy-done.4) | copy-start | bytes 1843204
  167.5 10.5 %copy-start.7 = (bf16[480,640]{1,0:T(8,128)(2,1)S(1)}, bf16[480,640]{1,0:T(8,128)(2,1)}, u32[]{:S(2)}) copy-start(bf16[480,640]{1,0:T(8,128)(2,1)} %copy-done.6) | copy-start | bytes 1843204
  188.9 8.7 %collective-permute-start.20 = (bf16[4,2,360,384]{3,2,0,1:T(8,128)(2,1)}, bf16[4,2,360,384]{3,2,0,1:T(8,128)(2,1)}, u32[]{:S(2)}, u32[]{:S(2)}) collective-permute-start(bf16[4,2,360,384]{3,2,0,1:T(8,128)(2,1)} %bitcast.138), channel_id=1, source_target_pairs={{0,1},{1,0},{2,3},{3,2},{4,5},{5,4},{6,7},{7,6},{8,9},{9,8},{10,11... | collective-permute-start | bytes 6635528 | tf_op jit(solution)/shard_map/ppermute | solution.py:233
  190.6 5.1 %collective-permute-start.31 = (bf16[2,576,640]{2,1,0:T(8,128)(2,1)}, bf16[2,576,640]{2,1,0:T(8,128)(2,1)}, u32[]{:S(2)}, u32[]{:S(2)}) collective-permute-start(bf16[2,576,640]{2,1,0:T(8,128)(2,1)} %fusion.5), channel_id=1, source_target_pairs={{0,1},{1,0},{2,3},{3,2},{4,5},{5,4},{6,7},{7,6},{8,9},{9,8},{10,11... | collective-permute-start | bytes 4423688 | tf_op jit(solution)/shard_map/ppermute | solution.py:233
  193.9 8.4 %collective-permute-start.25 = (bf16[4,2,360,256]{3,2,0,1:T(8,128)(2,1)}, bf16[4,2,360,256]{3,2,0,1:T(8,128)(2,1)}, u32[]{:S(2)}, u32[]{:S(2)}) collective-permute-start(bf16[4,2,360,256]{3,2,0,1:T(8,128)(2,1)} %bitcast.139), channel_id=1, source_target_pairs={{0,1},{1,0},{2,3},{3,2},{4,5},{5,4},{6,7},{7,6},{8,9},{9,8},{10,11... | collective-permute-start | bytes 4423688 | tf_op jit(solution)/shard_map/ppermute | solution.py:233
  195.7 2.1 copy-start.14
  200.1 2.3 copy-start.18
  200.1 27.4 %collective-permute-start.21 = (bf16[4,360,384]{2,1,0:T(8,128)(2,1)S(1)}, bf16[4,360,384]{2,1,0:T(8,128)(2,1)}, u32[]{:S(2)}, u32[]{:S(2)}) collective-permute-start(bf16[4,360,384]{2,1,0:T(8,128)(2,1)S(1)} %dynamic-slice_bitcast_fusion), channel_id=1, source_target_pairs={{0,2},{1,3},{2,0},{3,1},{4,6},{5,7},{6,4},{7,5},{8,10},{9,11},{10,... | collective-permute-start | bytes 3317768 | tf_op jit(solution)/shard_map/ppermute | solution.py:233
  200.8 18.3 %collective-permute-start.32 = (bf16[576,640]{1,0:T(8,128)(2,1)S(1)}, bf16[576,640]{1,0:T(8,128)(2,1)S(1)}, u32[]{:S(2)}, u32[]{:S(2)}) collective-permute-start(bf16[576,640]{1,0:T(8,128)(2,1)S(1)} %get-tuple-element.47), channel_id=1, source_target_pairs={{0,16},{16,0},{1,17},{17,1},{2,18},{18,2},{3,19},{19,3},{4,20},{20... | collective-permute-start | bytes 2211848 | tf_op jit(solution)/shard_map/ppermute | solution.py:237
  204.1 16.8 %copy-start.16 = (bf16[4,2,360,256]{3,2,0,1:T(8,128)(2,1)}, bf16[4,2,360,256]{3,2,0,1:T(8,128)(2,1)S(1)}, u32[]{:S(2)}) copy-start(bf16[4,2,360,256]{3,2,0,1:T(8,128)(2,1)S(1)} %fusion.2) | copy-start | bytes 4423684
  205.1 37.3 %collective-permute-start.26 = (bf16[4,360,256]{2,1,0:T(8,128)(2,1)}, bf16[4,360,256]{2,1,0:T(8,128)(2,1)}, u32[]{:S(2)}, u32[]{:S(2)}) collective-permute-start(bf16[4,360,256]{2,1,0:T(8,128)(2,1)} %dynamic-slice_bitcast_fusion.1), channel_id=1, source_target_pairs={{0,2},{1,3},{2,0},{3,1},{4,6},{5,7},{6,4},{7,5},{8,10},{9,11},{10,... | collective-permute-start | bytes 2211848 | tf_op jit(solution)/shard_map/ppermute | solution.py:233
  221.0 51.3 %collective-permute-start.33 = (bf16[2,576,640]{2,1,0:T(8,128)(2,1)}, bf16[2,576,640]{2,1,0:T(8,128)(2,1)}, u32[]{:S(2)}, u32[]{:S(2)}) collective-permute-start(bf16[2,576,640]{2,1,0:T(8,128)(2,1)} %get-tuple-element.45), channel_id=1, source_target_pairs={{0,1},{1,0},{2,3},{3,2},{4,5},{5,4},{6,7},{7,6},{8,9},{9,8},{10,11... | collective-permute-start | bytes 4423688 | tf_op jit(solution)/shard_map/ppermute | solution.py:233
  229.0 13.5 %copy-start.17 = (bf16[4,2,360,256]{3,2,0,1:T(8,128)(2,1)S(1)}, bf16[4,2,360,256]{3,2,0,1:T(8,128)(2,1)}, u32[]{:S(2)}) copy-start(bf16[4,2,360,256]{3,2,0,1:T(8,128)(2,1)} %copy-done.16) | copy-start | bytes 4423684
  229.1 21.0 %collective-permute-start.22 = (bf16[360,384]{1,0:T(8,128)(2,1)S(1)}, bf16[360,384]{1,0:T(8,128)(2,1)S(1)}, u32[]{:S(2)}, u32[]{:S(2)}) collective-permute-start(bf16[360,384]{1,0:T(8,128)(2,1)S(1)} %get-tuple-element.54), channel_id=1, source_target_pairs={{0,4},{1,5},{2,6},{3,7},{4,8},{5,9},{6,10},{7,11},{8,12},{9,13},{1... | collective-permute-start | bytes 829448 | tf_op jit(solution)/shard_map/ppermute | solution.py:233
  235.4 19.7 %collective-permute-start.23 = (bf16[360,384]{1,0:T(8,128)(2,1)S(1)}, bf16[360,384]{1,0:T(8,128)(2,1)S(1)}, u32[]{:S(2)}, u32[]{:S(2)}) collective-permute-start(bf16[360,384]{1,0:T(8,128)(2,1)S(1)} %get-tuple-element.56), channel_id=1, source_target_pairs={{0,8},{1,9},{2,10},{3,11},{4,12},{5,13},{6,14},{7,15},{8,0},{9,1},... | collective-permute-start | bytes 829448 | tf_op jit(solution)/shard_map/ppermute | solution.py:233
  235.4 33.6 %collective-permute-start.24 = (bf16[360,384]{1,0:T(8,128)(2,1)S(1)}, bf16[360,384]{1,0:T(8,128)(2,1)S(1)}, u32[]{:S(2)}, u32[]{:S(2)}) collective-permute-start(bf16[360,384]{1,0:T(8,128)(2,1)S(1)} %get-tuple-element.55), channel_id=1, source_target_pairs={{0,12},{1,13},{2,14},{3,15},{4,0},{5,1},{6,2},{7,3},{8,4},{9,5},{1... | collective-permute-start | bytes 829448 | tf_op jit(solution)/shard_map/ppermute | solution.py:233
  243.8 25.4 %collective-permute-start.27 = (bf16[360,256]{1,0:T(8,128)(2,1)S(1)}, bf16[360,256]{1,0:T(8,128)(2,1)S(1)}, u32[]{:S(2)}, u32[]{:S(2)}) collective-permute-start(bf16[360,256]{1,0:T(8,128)(2,1)S(1)} %get-tuple-element.59), channel_id=1, source_target_pairs={{0,4},{1,5},{2,6},{3,7},{4,8},{5,9},{6,10},{7,11},{8,12},{9,13},{1... | collective-permute-start | bytes 552968 | tf_op jit(solution)/shard_map/ppermute | solution.py:233
  250.1 19.1 %collective-permute-start.28 = (bf16[360,256]{1,0:T(8,128)(2,1)S(1)}, bf16[360,256]{1,0:T(8,128)(2,1)S(1)}, u32[]{:S(2)}, u32[]{:S(2)}) collective-permute-start(bf16[360,256]{1,0:T(8,128)(2,1)S(1)} %get-tuple-element.61), channel_id=1, source_target_pairs={{0,8},{1,9},{2,10},{3,11},{4,12},{5,13},{6,14},{7,15},{8,0},{9,1},... | collective-permute-start | bytes 552968 | tf_op jit(solution)/shard_map/ppermute | solution.py:233
  255.1 17.2 %copy-start.15 = (bf16[2,1,576,640]{3,2,0,1:T(8,128)(2,1)S(1)}, bf16[2,1,576,640]{3,2,0,1:T(8,128)(2,1)}, u32[]{:S(2)}) copy-start(bf16[2,1,576,640]{3,2,0,1:T(8,128)(2,1)} %get-tuple-element.44) | copy-start | bytes 4423684
  255.1 17.0 %collective-permute-start.29 = (bf16[360,256]{1,0:T(8,128)(2,1)S(1)}, bf16[360,256]{1,0:T(8,128)(2,1)S(1)}, u32[]{:S(2)}, u32[]{:S(2)}) collective-permute-start(bf16[360,256]{1,0:T(8,128)(2,1)S(1)} %get-tuple-element.60), channel_id=1, source_target_pairs={{0,12},{1,13},{2,14},{3,15},{4,0},{5,1},{6,2},{7,3},{8,4},{9,5},{1... | collective-permute-start | bytes 552968 | tf_op jit(solution)/shard_map/ppermute | solution.py:233
  276.4 11.6 %collective-permute-start.34 = (bf16[4,120,640]{2,1,0:T(8,128)(2,1)}, bf16[4,120,640]{2,1,0:T(8,128)(2,1)}, u32[]{:S(2)}, u32[]{:S(2)}) collective-permute-start(bf16[4,120,640]{2,1,0:T(8,128)(2,1)} %dynamic-slice_bitcast_fusion.3), channel_id=1, source_target_pairs={{0,2},{1,3},{2,0},{3,1},{4,6},{5,7},{6,4},{7,5},{8,10},{9,11},{10,... | collective-permute-start | bytes 1843208 | tf_op jit(solution)/shard_map/ppermute | solution.py:233
  277.6 6.8 %collective-permute-start.30 = (bf16[360,384]{1,0:T(8,128)(2,1)}, bf16[360,384]{1,0:T(8,128)(2,1)}, u32[]{:S(2)}, u32[]{:S(2)}) collective-permute-start(bf16[360,384]{1,0:T(8,128)(2,1)} %pad_maximum_fusion.14), channel_id=1, source_target_pairs={{0,16},{16,0},{1,17},{17,1},{2,18},{18,2},{3,19},{19,3},{4,20},{20... | collective-permute-start | bytes 829448 | tf_op jit(solution)/shard_map/ppermute | solution.py:237
  289.2 8.0 %collective-permute-start.35 = (bf16[120,640]{1,0:T(8,128)(2,1)S(1)}, bf16[120,640]{1,0:T(8,128)(2,1)S(1)}, u32[]{:S(2)}, u32[]{:S(2)}) collective-permute-start(bf16[120,640]{1,0:T(8,128)(2,1)S(1)} %get-tuple-element.66), channel_id=1, source_target_pairs={{0,4},{1,5},{2,6},{3,7},{4,8},{5,9},{6,10},{7,11},{8,12},{9,13},{1... | collective-permute-start | bytes 460808 | tf_op jit(solution)/shard_map/ppermute | solution.py:233
  292.2 8.9 %collective-permute-start.36 = (bf16[120,640]{1,0:T(8,128)(2,1)S(1)}, bf16[120,640]{1,0:T(8,128)(2,1)S(1)}, u32[]{:S(2)}, u32[]{:S(2)}) collective-permute-start(bf16[120,640]{1,0:T(8,128)(2,1)S(1)} %get-tuple-element.68), channel_id=1, source_target_pairs={{0,8},{1,9},{2,10},{3,11},{4,12},{5,13},{6,14},{7,15},{8,0},{9,1},... | collective-permute-start | bytes 460808 | tf_op jit(solution)/shard_map/ppermute | solution.py:233
  294.5 6.9 %collective-permute-start.37 = (bf16[120,640]{1,0:T(8,128)(2,1)S(1)}, bf16[120,640]{1,0:T(8,128)(2,1)S(1)}, u32[]{:S(2)}, u32[]{:S(2)}) collective-permute-start(bf16[120,640]{1,0:T(8,128)(2,1)S(1)} %get-tuple-element.67), channel_id=1, source_target_pairs={{0,12},{1,13},{2,14},{3,15},{4,0},{5,1},{6,2},{7,3},{8,4},{9,5},{1... | collective-permute-start | bytes 460808 | tf_op jit(solution)/shard_map/ppermute | solution.py:233

commit v2 on v1

--- a/solution.py
+++ b/solution.py
@@ -251,41 +251,47 @@
     )
 
 
-def place_blocks(place_ref, blocks_ref, out_ref):
-    rows = blocks_ref.shape[1]
-    for block in range(blocks_ref.shape[0]):
-        start = pl.multiple_of(place_ref[block] * rows, 16)
-        out_ref[pl.ds(start, rows), :] = blocks_ref[block]
-
-
-def gathered(value):
-    rows, lanes = value.shape
+def after(value, earlier):
+    return value if earlier is None else lax.optimization_barrier((value, earlier))[0]
+
+
+def in_order(swap, own, other, axis):
+    return jnp.where(
+        swap, jnp.concatenate([other, own], axis), jnp.concatenate([own, other], axis)
+    )
+
+
+def over_z(value, pairs):
+    moves = []
+    for source, target in pairs:
+        for rest in range(GRID[1] * GRID[2]):
+            moves.append(tuple(z * GRID[1] * GRID[2] + rest for z in (source, target)))
+    return lax.ppermute(value, "dp", moves)
+
+
+def gathered(values):
     z, y, c = coordinates()
-    line = jnp.stack([value] + [shifted(value, dz=step) for step in range(1, GRID[0])])
-    plane = jnp.stack([line, shifted(line, dy=1)])
-    other = shifted(plane, dc=1)
-    pair = jnp.where(c == 0, jnp.stack([plane, other], 2), jnp.stack([other, plane], 2))
-    blocks = pair.reshape(GRID[0] * GRID[1], GRID[2] * rows, lanes)
-    places = jnp.stack(
-        [
-            ((z - step) % GRID[0]) * GRID[1] + (y + dy) % GRID[1]
-            for dy in range(GRID[1])
-            for step in range(GRID[0])
-        ]
-    ).astype(jnp.int32)
-    total = GRID[0] * GRID[1] * GRID[2] * rows
-    return pl.pallas_call(
-        place_blocks,
-        out_shape=jax.ShapeDtypeStruct((total, lanes), value.dtype),
-        in_specs=[
-            pl.BlockSpec(memory_space=pltpu.SMEM),
-            pl.BlockSpec(memory_space=pltpu.VMEM),
-        ],
-        compiler_params=pltpu.CompilerParams(vmem_limit_bytes=40 * 2**20),
-        cost_estimate=pl.CostEstimate(
-            flops=0, bytes_accessed=4 * total * lanes, transcendentals=0
-        ),
-    )(places, blocks)
+    pair_sent, sides = None, []
+    results = []
+    for chunk, value in enumerate(values):
+        rows, lanes = value.shape
+        pair_sent = over_z(after(value, pair_sent), [(0, 1), (1, 0), (2, 3), (3, 2)])
+        near = in_order(z % 2 == 1, value[None], pair_sent[None], 0)
+        middle = over_z(near, [(1, 2), (2, 1)])
+        outer = over_z(middle, [(1, 0), (2, 3)])
+        far = jnp.where((z == 1) | (z == 2), middle, outer)
+        if chunk == 0:
+            side = [shifted(near, dy=1), shifted(far, dy=1)]
+            line = in_order(z >= 2, near, far, 0)
+            side = in_order(z >= 2, side[0], side[1], 0)
+        else:
+            line = in_order(z >= 2, near, far, 0)
+            side = shifted(after(line, sides[-2] if len(sides) > 1 else None), dy=1)
+        sides.append(side)
+        plane = in_order(y == 1, line[:, None], side[:, None], 1)
+        whole = in_order(c == 1, plane[:, :, None], shifted(plane, dc=1)[:, :, None], 2)
+        results.append(whole.reshape(-1, lanes))
+    return results
 
 
 def added(*terms):
@@ -298,19 +304,14 @@
     return added(part_of(value, c, 2), sent).astype(BF16)
 
 
-def summed_over_chips(value):
+def summed_over_chips(value, earlier):
     z, y, _ = coordinates()
-    sent = shifted(part_of(value, 1 - y, 1), dy=1)
+    sent = shifted(after(part_of(value, 1 - y, 1), earlier), dy=1)
     line = added(part_of(value, y, 1), sent).astype(BF16)
     terms = [part_of(line, z, 0)] + [
         shifted(part_of(line, (z + step) % GRID[0], 0), dz=step) for step in range(1, GRID[0])
     ]
-    return added(*terms)
-
-
-def scattered(value):
-    lanes = value.shape[1]
-    return summed_over_chips(summed_on_chip(value.reshape(*GRID, -1, lanes)))
+    return added(*terms), sent
 
 
 def pixel_masks(rows):
@@ -360,27 +361,33 @@
     return logistic, preact * logistic
 
 
-def convolved(normed, weight_ref, masks):
+def tap_weight(weight_refs, tap, channels):
+    return jnp.concatenate(
+        [ref[tap * channels : (tap + 1) * channels, :] for ref in weight_refs], 1
+    )
+
+
+def convolved(normed, weight_refs, masks):
     rows, channels = normed.shape
     normed = normed.astype(F32)
     total = None
     for tap in range(9):
         term = dot(
             moved_rows(normed, masks[tap]).astype(BF16),
-            weight_ref[tap * channels : (tap + 1) * channels, :],
+            tap_weight(weight_refs, tap, channels),
         )
         total = term if total is None else total + term
     return total
 
 
-def first_forward(frames, hidden_ref, embedding_ref, keep_ref, spatial_ref, temporal_ref, *outs):
-    normed_ref, preact_ref, mixed_ref = outs
+def first_forward(frames, hidden_ref, embedding_ref, keep_ref, temporal_ref, *refs):
+    *spatial_refs, normed_ref, preact_ref, mixed_ref = refs
     rows = hidden_ref.shape[0]
     width = keep_ref.shape[1]
     summed = with_embedding(hidden_ref[...].astype(F32), embedding_ref, embedding_ref.shape[0])
     normed = (summed * scale_of(summed)).astype(BF16)
     normed_ref[...] = normed
-    preact = convolved(normed, spatial_ref, pixel_masks(rows))
+    preact = convolved(normed, spatial_refs, pixel_masks(rows))
     preact_ref[...] = preact
     activated = silu_parts(preact)[1].astype(BF16).astype(F32) * keep_ref[...]
     mixed = None
@@ -422,20 +429,24 @@
         ).astype(BF16)
 
 
-def store_spatial_terms(normed, pre_grad, out_ref):
+def store_spatial_terms(normed, pre_grad, out_refs):
     channels = normed.shape[1]
     pre_grad = pre_grad.astype(F32)
     masks = pixel_masks(pre_grad.shape[0])
     for tap in range(9):
-        out_ref[tap * channels : (tap + 1) * channels, :] = dot(
+        term = dot(
             normed, moved_rows(pre_grad, masks[8 - tap]).astype(BF16), ((0,), (0,))
         ).astype(BF16)
+        for tile, out_ref in enumerate(out_refs):
+            out_ref[tap * channels : (tap + 1) * channels, :] = term[
+                :, tile * LANES : (tile + 1) * LANES
+            ]
 
 
 def second_forward(
-    frames, hidden_ref, own_ref, sent_ref, embedding_ref, keep_ref, upstream_ref, spatial_ref,
-    temporal_ref, next_ref, normed_ref, activated_ref, pre_grad_ref, back_ref,
+    frames, hidden_ref, own_ref, sent_ref, embedding_ref, keep_ref, upstream_ref, temporal_ref, *refs
 ):
+    *spatial_refs, next_ref, normed_ref, activated_ref, pre_grad_ref, back_ref = refs
     rows, channels = hidden_ref.shape
     width = keep_ref.shape[1]
     masks = pixel_masks(rows)
@@ -445,7 +456,7 @@
     summed = with_embedding(hidden.astype(F32), embedding_ref, embedding_ref.shape[0])
     normed = (summed * scale_of(summed)).astype(BF16)
     normed_ref[...] = normed
-    preact = convolved(normed, spatial_ref, masks)
+    preact = convolved(normed, spatial_refs, masks)
     activated_ref[...] = (silu_parts(preact)[1] * keep_ref[...]).astype(BF16)
     act_grad = act_grad_of(upstream_ref[...], temporal_ref, width, frames)
     pre_grad = (act_grad * slope_of(preact) * keep_ref[...]).astype(BF16)
@@ -455,7 +466,7 @@
     for tap in range(9):
         term = dot(
             moved_rows(pre_grad, masks[8 - tap]).astype(BF16),
-            spatial_ref[tap * channels : (tap + 1) * channels, :],
+            tap_weight(spatial_refs, tap, channels),
             ((1,), (1,)),
         )
         back = term if back is None else back + term
@@ -463,15 +474,16 @@
 
 
 def second_terms(frames, normed_ref, pre_grad_ref, activated_ref, upstream_ref, *outs):
-    spatial_ref, temporal_ref = outs
-    store_spatial_terms(normed_ref[...], pre_grad_ref[...], spatial_ref)
+    *spatial_refs, temporal_ref = outs
+    store_spatial_terms(normed_ref[...], pre_grad_ref[...], spatial_refs)
     store_temporal_terms(activated_ref[...], upstream_ref[...], frames, temporal_ref)
 
 
 def first_terms(
     frames, hidden_ref, embedding_ref, upstream_ref, own_ref, sent_ref, normed_ref, preact_ref,
-    keep_ref, temporal_ref, spatial_out, temporal_out,
+    keep_ref, temporal_ref, *outs
 ):
+    *spatial_outs, temporal_out = outs
     width = keep_ref.shape[1]
     channels = hidden_ref.shape[1]
     summed = with_embedding(hidden_ref[...].astype(F32), embedding_ref, embedding_ref.shape[0])
@@ -484,7 +496,7 @@
     activated = (silu_parts(preact)[1] * keep_ref[...]).astype(BF16)
     act_grad = act_grad_of(upstream, temporal_ref, width, frames)
     pre_grad = (act_grad * slope_of(preact) * keep_ref[...]).astype(BF16)
-    store_spatial_terms(normed_ref[...], pre_grad, spatial_out)
+    store_spatial_terms(normed_ref[...], pre_grad, spatial_outs)
     store_temporal_terms(activated, upstream, frames, temporal_out)
 
 
@@ -509,16 +521,27 @@
     def main_of(value, index, axis):
         return lax.dynamic_slice_in_dim(value, index * main, main, axis)
 
-    temporal_own = gathered(temporal_weight[0]).reshape(3, channels, channels)
     spatial_own = spatial_weight[0]
     given = swapped(
         jnp.concatenate([main_of(spatial_own, 1 - me, 1), spatial_own[:, 2 * main :]], 1)
     )
     main_own, main_given = main_of(spatial_own, me, 1), given[:, :main]
     tails = jnp.where(tail, spatial_own[:, 2 * main :], given[:, main:])
-    spatial_first = gathered(jnp.concatenate([jnp.where(first, main_own, main_given), tails], 1))
-    main_second = gathered(jnp.where(first, main_given, main_own))
-    spatial_second = jnp.concatenate([main_second, spatial_first[:, main:]], 1)
+    main_first = jnp.where(first, main_own, main_given)
+    main_second = jnp.where(first, main_given, main_own)
+    temporal_own, *mains_first, tails, low, high = gathered(
+        [
+            temporal_weight[0],
+            main_first[:, :LANES],
+            main_first[:, LANES:],
+            tails,
+            main_second[:, :LANES],
+            main_second[:, LANES:],
+        ]
+    )
+    temporal_own = temporal_own.reshape(3, channels, channels)
+    spatial_first = [*mains_first, tails]
+    spatial_second = [low, high, tails]
 
     def local_rows(index):
         return jnp.concatenate(
@@ -546,7 +569,7 @@
         (shape((rows, channels)), shape((rows, width), F32), shape((rows, channels))),
         flops=spatial_flops + temporal_flops,
         moved=spatial_bytes + temporal_bytes,
-    )(hidden, embedding, keep_first, spatial_first, temporal_first)
+    )(hidden, embedding, keep_first, temporal_first, *spatial_first)
     hidden_second, normed_second, activated_second, pre_grad_second, back = vmem_call(
         functools.partial(second_forward, frames),
         (
@@ -559,29 +582,37 @@
         flops=2 * spatial_flops + temporal_flops,
         moved=spatial_bytes + temporal_bytes,
     )(
-        hidden, mixed, swapped(mixed), embedding, keep_second, upstream, spatial_second,
-        temporal_second,
-    )
+        hidden, mixed, swapped(mixed), embedding, keep_second, upstream, temporal_second,
+        *spatial_second,
+    )
+
+    def terms_shape():
+        return (shape((9 * channels, LANES)),) * 3 + (shape((3 * width, channels)),)
 
     back_given = swapped(back)
-    spatial_terms_second, temporal_terms_second = vmem_call(
+    *spatial_terms_second, temporal_terms_second = vmem_call(
         functools.partial(second_terms, frames),
-        (shape((9 * channels, width)), shape((3 * width, channels))),
+        terms_shape(),
         flops=spatial_flops + temporal_flops,
         moved=spatial_bytes + temporal_bytes,
     )(normed_second, pre_grad_second, activated_second, upstream)
-    grad_second = scattered(spatial_terms_second[:, :main])
-    spatial_terms_first, temporal_terms_first = vmem_call(
+    *spatial_terms_first, temporal_terms_first = vmem_call(
         functools.partial(first_terms, frames),
-        (shape((9 * channels, width)), shape((3 * width, channels))),
+        terms_shape(),
         flops=spatial_flops + 2 * temporal_flops,
         moved=spatial_bytes + 2 * temporal_bytes,
     )(
         hidden_second, embedding, upstream, back, back_given, normed_first, preact_first,
         keep_first, temporal_first,
     )
-    tail_terms = spatial_terms_first[:, main:] + spatial_terms_second[:, main:]
-    grad_first = scattered(jnp.concatenate([spatial_terms_first[:, :main], tail_terms], 1))
+    tail_terms = spatial_terms_first[2] + spatial_terms_second[2]
+    sides, shares = [None, None], []
+    for terms in (*spatial_terms_second[:2], tail_terms, *spatial_terms_first[:2]):
+        share, side = summed_over_chips(
+            summed_on_chip(terms.reshape(*GRID, -1, LANES)), sides[-2]
+        )
+        sides.append(side)
+        shares.append(share)
 
     terms = jnp.stack(
         [
@@ -607,16 +638,23 @@
         ],
         1,
     )
-    share_temporal = summed_over_chips(part_of(full.reshape(*GRID, -1, channels), c, 2))
-
-    kept = jnp.where(first, grad_first[:, :main], grad_second)
-    passed = jnp.where(first, grad_second, grad_first[:, :main])
-    given = swapped(jnp.concatenate([passed, grad_first[:, main:]], 1).astype(BF16)).astype(F32)
+    share_temporal, _ = summed_over_chips(
+        part_of(full.reshape(*GRID, -1, channels), c, 2), sides[-2]
+    )
+
+    share_second, share_tails, share_first = (
+        jnp.concatenate(shares[:2], 1),
+        shares[2],
+        jnp.concatenate(shares[3:], 1),
+    )
+    kept = jnp.where(first, share_first, share_second)
+    passed = jnp.where(first, share_second, share_first)
+    given = swapped(jnp.concatenate([passed, share_tails], 1).astype(BF16)).astype(F32)
     share_spatial = jnp.concatenate(
         [
             jnp.where(first, kept, given[:, :main]),
             jnp.where(first, given[:, :main], kept),
-            jnp.where(tail, grad_first[:, main:], given[:, main:]),
+            jnp.where(tail, share_tails, given[:, main:]),
         ],
         1,
     )

time: 309 us -> 267 us (0.86)
  other arithmetic: 36 us -> 18.5 us
  starting transfers between devices: 84.6 us -> 76.7 us
  local copies, waits for them, and re-layouts: 19.6 us -> 12.6 us
  waiting for transfers between devices: 132 us -> 127 us
    ppermute x32 -> x45, starting transfers between devices: 75.3 us -> 44.2 us  [shifted(): return lax.ppermute(value, 'dp', pairs)]
    ppermute x0 -> x18, starting transfers between devices: none -> 24.4 us  [over_z(): return lax.ppermute(value, 'dp', moves)]
    ppermute x0 -> x18, waiting for transfers between devices: none -> 23.1 us  [over_z(): return lax.ppermute(value, 'dp', moves)]
    ppermute x6, waiting for transfers between devices: 54.7 us -> 35.3 us  [swapped(): return lax.ppermute(value, 'pipe', [(0, 1), (1, 0)])]
    ppermute x32 -> x45, waiting for transfers between devices: 77.7 us -> 68.3 us  [shifted(): return lax.ppermute(value, 'dp', pairs)]
    another operation x8 -> x2, other arithmetic: 7.18 us -> 0.11 us  [the longest x3 4.27 us: gathered(): jnp.stack([plane, other], 2)]
    dynamic_slice x4 -> x8, local copies, waits for them, and re-layouts: 5.99 us -> 1.05 us  [part_of(): return lax.dynamic_index_in_dim(value, index, axis, keepdims=False)]
    pallas_call x5 -> x2, Pallas kernels: 13.4 us -> 11.1 us  [the longest x1 6.78 us: paired_device(): vmem_call(functools.partial(first_terms, frames), terms_shape(), flops=sp...]
  transfers between devices with their start and end apart: 38 -> 69, of which waited for: 18 -> 30; matrix products, arithmetic and copies ran while one was open for 11% -> 7% of each run, Pallas kernels for 2% -> 4%
where the time goes in v2:
time: 267 us; the launch traced here: 263 us
  waiting for transfers between devices  127 us (48%)
  starting transfers between devices  76.7 us (29%)
  Pallas kernels  25.9 us (10%)
  other arithmetic  18.5 us (7%)
  local copies, waits for them, and re-layouts  12.6 us (5%)
    ppermute x45, waiting for transfers between devices, shifted(): return lax.ppermute(value, 'dp', pairs)  68.3 us
    ppermute x45, starting transfers between devices, shifted(): return lax.ppermute(value, 'dp', pairs)  44.2 us
    ppermute x6, waiting for transfers between devices, swapped(): return lax.ppermute(value, 'pipe', [(0, 1), (1, 0)])  35.3 us
    ppermute x18, starting transfers between devices, over_z(): return lax.ppermute(value, 'dp', moves)  24.4 us
    ppermute x18, waiting for transfers between devices, over_z(): return lax.ppermute(value, 'dp', moves)  23.1 us
    pallas_call x1, Pallas kernels, paired_device(): vmem_call(functools.partial(second_forward, frames), (shape((rows, channe...  8.64 us
    ppermute x6, starting transfers between devices, swapped(): return lax.ppermute(value, 'pipe', [(0, 1), (1, 0)])  8.09 us
    unnamed x42, local copies, waits for them, and re-layouts  7.04 us
  transfers between devices with their start and end apart: 69, of which 30 were waited for; matrix products, arithmetic and copies ran while one was open for 7% of the time, Pallas kernels for 4%

profile of v2, /device:TPU:0, one launch (start us, length us, event | category | flops | bytes accessed | tf_op | source)
XLA Modules:
  0.0 262.6 jit_solution(2265017018378616889)
XLA Ops:
  0.7 3.1 %collective-permute-start = (bf16[120,640]{1,0:T(8,128)(2,1)}, bf16[120,640]{1,0:T(8,128)(2,1)S(1)}, u32[]{:S(2)}, u32[]{:S(2)}) collective-permute-start(bf16[120,640]{1,0:T(8,128)(2,1)} %bitcast.305), channel_id=1, source_target_pairs={{0,4},{1,5},{2,6},{3,7},{4,0},{5,1},{6,2},{7,3},{8,12},{9,13},{10,... | collective-permute-start | bytes 460808 | tf_op jit(solution)/shard_map/ppermute | solution.py:269
  5.6 1.6 collective-permute-start.8
  8.2 1.1 maximum_select_fusion.32
  9.3 1.6 collective-permute-start.4
  11.6 2.1 collective-permute-done.8
  13.9 2.4 collective-permute-start.9
  16.4 2.4 collective-permute-done.9
  18.8 2.0 collective-permute-start.14
  21.6 1.3 collective-permute-start.2
  23.4 2.3 collective-permute-start.19
  26.4 1.3 collective-permute-start.11
  27.8 7.5 %collective-permute-done.19 = bf16[360,128]{1,0:T(8,128)(2,1)S(1)} collective-permute-done((bf16[360,128]{1,0:T(8,128)(2,1)S(1)}, bf16[360,128]{1,0:T(8,128)(2,1)S(1)}, u32[]{:S(2)}, u32[]{:S(2)}) %collective-permute-start.19) | collective-permute-done | bytes 92192 | tf_op jit(solution)/shard_map/ppermute | solution.py:269
  36.0 4.3 %collective-permute-done.25 = bf16[360,128]{1,0:T(8,128)(2,1)S(1)} collective-permute-done((bf16[360,128]{1,0:T(8,128)(2,1)S(1)}, bf16[360,128]{1,0:T(8,128)(2,1)S(1)}, u32[]{:S(2)}, u32[]{:S(2)}) %collective-permute-start.25) | collective-permute-done | bytes 92192 | tf_op jit(solution)/shard_map/ppermute | solution.py:269
  40.3 1.3 collective-permute-start.16
  41.7 2.7 %collective-permute-start.30 = (bf16[360,128]{1,0:T(8,128)(2,1)S(1)}, bf16[360,128]{1,0:T(8,128)(2,1)S(1)}, u32[]{:S(2)}, u32[]{:S(2)}) collective-permute-start(bf16[360,128]{1,0:T(8,128)(2,1)S(1)} %get-tuple-element.37), channel_id=1, source_target_pairs={{0,4},{1,5},{2,6},{3,7},{4,0},{5,1},{6,2},{7,3},{8,12},{9,13},{10,... | collective-permute-start | bytes 276488 | tf_op jit(solution)/shard_map/ppermute | solution.py:269
  44.5 4.2 %collective-permute-done.30 = bf16[360,128]{1,0:T(8,128)(2,1)S(1)} collective-permute-done((bf16[360,128]{1,0:T(8,128)(2,1)S(1)}, bf16[360,128]{1,0:T(8,128)(2,1)S(1)}, u32[]{:S(2)}, u32[]{:S(2)}) %collective-permute-start.30) | collective-permute-done | bytes 92192 | tf_op jit(solution)/shard_map/ppermute | solution.py:269
  49.5 1.9 collective-permute-start.12
  51.4 1.3 collective-permute-start.21
  53.9 1.9 collective-permute-start.17
  55.9 8.6 %collective-permute-done.3 = bf16[2,120,640]{2,1,0:T(8,128)(2,1)S(1)} collective-permute-done((bf16[2,120,640]{2,1,0:T(8,128)(2,1)S(1)}, bf16[2,120,640]{2,1,0:T(8,128)(2,1)S(1)}, u32[]{:S(2)}, u32[]{:S(2)}) %collective-permute-start.3) | collective-permute-done | bytes 307232 | tf_op jit(solution)/shard_map/ppermute | solution.py:233
  64.4 1.3 collective-permute-start.27
  66.3 1.5 collective-permute-start.32
  67.8 4.3 %collective-permute-done.27 = bf16[2,360,128]{2,1,0:T(8,128)(2,1)S(1)} collective-permute-done((bf16[2,360,128]{2,1,0:T(8,128)(2,1)S(1)}, bf16[2,360,128]{2,1,0:T(8,128)(2,1)S(1)}, u32[]{:S(2)}, u32[]{:S(2)}) %collective-permute-start.27) | collective-permute-done | bytes 184352 | tf_op jit(solution)/shard_map/ppermute | solution.py:269
  72.6 1.4 collective-permute-start.22
  75.8 1.6 collective-permute-start.6
  78.2 1.9 collective-permute-done.22
  80.5 7.8 %collective-permute-done.28 = bf16[4,360,128]{2,1,0:T(8,128)(2,1)S(1)} collective-permute-done((bf16[4,360,128]{2,1,0:T(8,128)(2,1)S(1)}, bf16[4,360,128]{2,1,0:T(8,128)(2,1)S(1)}, u32[]{:S(2)}, u32[]{:S(2)}) %collective-permute-start.28) | collective-permute-done | bytes 368672 | tf_op jit(solution)/shard_map/ppermute | solution.py:233
  88.3 1.2 collective-permute-start.33
  89.4 5.3 %collective-permute-done.6 = bf16[576,640]{1,0:T(8,128)(2,1)S(1)} collective-permute-done((bf16[576,640]{1,0:T(8,128)(2,1)S(1)}, bf16[576,640]{1,0:T(8,128)(2,1)S(1)}, u32[]{:S(2)}, u32[]{:S(2)}) %collective-permute-start.6) | collective-permute-done | bytes 737312 | tf_op jit(solution)/shard_map/ppermute | solution.py:237
  95.9 2.2 collective-permute-done.33
  100.2 6.2 %shard_map.68 = (bf16[480,640]{1,0:T(8,128)(2,1)S(1)}, f32[480,384]{1,0:T(8,128)S(1)}, bf16[480,640]{1,0:T(8,128)(2,1)S(1)}) custom-call(bf16[480,640]{1,0:T(8,128)(2,1)S(1)} %bitcast.246, f32[5,640]{1,0:T(8,128)S(1)} %pad_maximum_fusion.8.embedding_ref, f32[1,384]{1,0:T(1,128)S(1)} %select_n.721.keep_ref, ...), custom_call_target="tpu_custom_call" | custom-call | flops 2831155200 | bytes 5898240 | tf_op jit(solution)/shard_map/pallas_call | solution.py:567
  106.3 1.4 collective-permute-start.24
  108.7 13.9 %collective-permute-done.24.sent_ref = bf16[480,640]{1,0:T(8,128)(2,1)S(1)} collective-permute-done((bf16[480,640]{1,0:T(8,128)(2,1)S(1)}, bf16[480,640]{1,0:T(8,128)(2,1)S(1)}, u32[]{:S(2)}, u32[]{:S(2)}) %collective-permute-start.24) | collective-permute-done | bytes 614432 | tf_op jit(solution)/shard_map/ppermute | solution.py:237
  122.7 8.6 %shard_map.69 = (bf16[480,640]{1,0:T(8,128)(2,1)S(1)}, bf16[480,640]{1,0:T(8,128)(2,1)S(1)}, bf16[480,384]{1,0:T(8,128)(2,1)S(1)}, bf16[480,384]{1,0:T(8,128)(2,1)S(1)}, bf16[480,640]{1,0:T(8,128)(2,1)S(1)}) custom-call(bf16[480,640]{1,0:T(8,128)(2,1)S(1)} %bitcast.247, bf16[480,640]{1,0:T(8,128)(2,1)S(1)} %get-tuple-element.34.own_ref, ...), custom_call_target="tpu_custom_call" | custom-call | flops 4954521600 | bytes 5898240 | tf_op jit(solution)/shard_map/pallas_call | solution.py:573
  134.5 1.3 collective-permute-start.35
  135.8 1.1 copy-done.9
  138.8 4.4 %shard_map.71 = (bf16[5760,128]{1,0:T(8,128)(2,1)S(1)}, bf16[5760,128]{1,0:T(8,128)(2,1)S(1)}, bf16[5760,128]{1,0:T(8,128)(2,1)S(1)}, bf16[1152,640]{1,0:T(8,128)(2,1)S(1)}) custom-call(bf16[480,640]{1,0:T(8,128)(2,1)S(1)} %copy-done.9, bf16[480,384]{1,0:T(8,128)(2,1)S(1)} %copy-done.13, bf16[480,384]{1,0:T(8,128)(2,1)S(1)} %copy-done.11, ...), custom_call_target="tpu_custom_call" | custom-call | flops 2831155200 | bytes 5898240 | tf_op jit(solution)/shard_map/pallas_call | solution.py:593
  143.2 6.8 %collective-permute-done.35.sent_ref = bf16[480,640]{1,0:T(8,128)(2,1)S(1)} collective-permute-done((bf16[480,640]{1,0:T(8,128)(2,1)S(1)}, bf16[480,640]{1,0:T(8,128)(2,1)S(1)}, u32[]{:S(2)}, u32[]{:S(2)}) %collective-permute-start.35) | collective-permute-done | bytes 614432 | tf_op jit(solution)/shard_map/ppermute | solution.py:237
  149.9 6.8 %shard_map.70 = (bf16[5760,128]{1,0:T(8,128)(2,1)S(1)}, bf16[5760,128]{1,0:T(8,128)(2,1)S(1)}, bf16[5760,128]{1,0:T(8,128)(2,1)S(1)}, bf16[1152,640]{1,0:T(8,128)(2,1)S(1)}) custom-call(bf16[480,640]{1,0:T(8,128)(2,1)S(1)} %copy-done.7, f32[5,640]{1,0:T(8,128)S(1)} %pad_maximum_fusion.8.embedding_ref, bf16[480,640]{1,0:T(8,128)(2,1)S(1)} %bitcast.250, ...), custom_call_target="tpu_custom_call" | custom-call | flops 3538944000 | bytes 7372800 | tf_op jit(solution)/shard_map/pallas_call | solution.py:599
  159.9 1.9 collective-permute-done.45
  162.8 1.3 collective-permute-start.46
  165.9 8.3 %collective-permute-done.46 = bf16[4,360,128]{2,1,0:T(8,128)(2,1)S(1)} collective-permute-done((bf16[4,360,128]{2,1,0:T(8,128)(2,1)S(1)}, bf16[4,360,128]{2,1,0:T(8,128)(2,1)S(1)}, u32[]{:S(2)}, u32[]{:S(2)}) %collective-permute-start.46) | collective-permute-done | bytes 368672 | tf_op jit(solution)/shard_map/ppermute | solution.py:233
  175.1 3.2 %collective-permute-start.54 = (bf16[360,128]{1,0:T(8,128)(2,1)S(1)}, bf16[360,128]{1,0:T(8,128)(2,1)S(1)}, u32[]{:S(2)}, u32[]{:S(2)}) collective-permute-start(bf16[360,128]{1,0:T(8,128)(2,1)S(1)} %get-tuple-element.98), channel_id=1, source_target_pairs={{0,12},{1,13},{2,14},{3,15},{4,0},{5,1},{6,2},{7,3},{8,4},{9,5},{1... | collective-permute-start | bytes 276488 | tf_op jit(solution)/shard_map/ppermute | solution.py:233
  178.2 3.3 %collective-permute-done.38 = bf16[4,360,128]{2,1,0:T(8,128)(2,1)S(1)} collective-permute-done((bf16[4,360,128]{2,1,0:T(8,128)(2,1)S(1)}, bf16[4,360,128]{2,1,0:T(8,128)(2,1)S(1)}, u32[]{:S(2)}, u32[]{:S(2)}) %collective-permute-start.38) | collective-permute-done | bytes 368672 | tf_op jit(solution)/shard_map/ppermute | solution.py:233
  182.4 3.2 %collective-permute-start.57 = (bf16[360,128]{1,0:T(8,128)(2,1)S(1)}, bf16[360,128]{1,0:T(8,128)(2,1)S(1)}, u32[]{:S(2)}, u32[]{:S(2)}) collective-permute-start(bf16[360,128]{1,0:T(8,128)(2,1)S(1)} %get-tuple-element.101), channel_id=1, source_target_pairs={{0,12},{1,13},{2,14},{3,15},{4,0},{5,1},{6,2},{7,3},{8,4},{9,5},{1... | collective-permute-start | bytes 276488 | tf_op jit(solution)/shard_map/ppermute | solution.py:233
  186.2 1.3 collective-permute-start.39
  189.2 1.3 collective-permute-start.47
  190.5 2.4 collective-permute-done.56
  193.0 4.9 %collective-permute-done.39 = bf16[4,360,128]{2,1,0:T(8,128)(2,1)S(1)} collective-permute-done((bf16[4,360,128]{2,1,0:T(8,128)(2,1)S(1)}, bf16[4,360,128]{2,1,0:T(8,128)(2,1)S(1)}, u32[]{:S(2)}, u32[]{:S(2)}) %collective-permute-start.39) | collective-permute-done | bytes 368672 | tf_op jit(solution)/shard_map/ppermute | solution.py:233
  198.7 3.1 %collective-permute-start.42 = (bf16[360,128]{1,0:T(8,128)(2,1)S(1)}, bf16[360,128]{1,0:T(8,128)(2,1)S(1)}, u32[]{:S(2)}, u32[]{:S(2)}) collective-permute-start(bf16[360,128]{1,0:T(8,128)(2,1)S(1)} %get-tuple-element.92), channel_id=1, source_target_pairs={{0,12},{1,13},{2,14},{3,15},{4,0},{5,1},{6,2},{7,3},{8,4},{9,5},{1... | collective-permute-start | bytes 276488 | tf_op jit(solution)/shard_map/ppermute | solution.py:233
  201.8 1.0 collective-permute-start.41
  203.7 1.3 collective-permute-start.48
  206.0 3.5 %collective-permute-start.60 = (bf16[360,128]{1,0:T(8,128)(2,1)S(1)}, bf16[360,128]{1,0:T(8,128)(2,1)S(1)}, u32[]{:S(2)}, u32[]{:S(2)}) collective-permute-start(bf16[360,128]{1,0:T(8,128)(2,1)S(1)} %get-tuple-element.104), channel_id=1, source_target_pairs={{0,12},{1,13},{2,14},{3,15},{4,0},{5,1},{6,2},{7,3},{8,4},{9,5},{1... | collective-permute-start | bytes 276488 | tf_op jit(solution)/shard_map/ppermute | solution.py:233
  210.3 1.9 collective-permute-done.48
  212.7 3.5 %collective-permute-start.51 = (bf16[360,128]{1,0:T(8,128)(2,1)S(1)}, bf16[360,128]{1,0:T(8,128)(2,1)S(1)}, u32[]{:S(2)}, u32[]{:S(2)}) collective-permute-start(bf16[360,128]{1,0:T(8,128)(2,1)S(1)} %get-tuple-element.95), channel_id=1, source_target_pairs={{0,12},{1,13},{2,14},{3,15},{4,0},{5,1},{6,2},{7,3},{8,4},{9,5},{1... | collective-permute-start | bytes 276488 | tf_op jit(solution)/shard_map/ppermute | solution.py:233
  217.1 4.3 %collective-permute-done.59 = bf16[360,128]{1,0:T(8,128)(2,1)S(1)} collective-permute-done((bf16[360,128]{1,0:T(8,128)(2,1)S(1)}, bf16[360,128]{1,0:T(8,128)(2,1)S(1)}, u32[]{:S(2)}, u32[]{:S(2)}) %collective-permute-start.59) | collective-permute-done | bytes 92192 | tf_op jit(solution)/shard_map/ppermute | solution.py:233
  221.4 4.8 %collective-permute-done.50 = bf16[360,128]{1,0:T(8,128)(2,1)S(1)} collective-permute-done((bf16[360,128]{1,0:T(8,128)(2,1)S(1)}, bf16[360,128]{1,0:T(8,128)(2,1)S(1)}, u32[]{:S(2)}, u32[]{:S(2)}) %collective-permute-start.50) | collective-permute-done | bytes 92192 | tf_op jit(solution)/shard_map/ppermute | solution.py:233
  230.7 1.3 collective-permute-start.61
  232.0 7.2 %collective-permute-done.61 = bf16[360,384]{1,0:T(8,128)(2,1)} collective-permute-done((bf16[360,384]{1,0:T(8,128)(2,1)}, bf16[360,384]{1,0:T(8,128)(2,1)}, u32[]{:S(2)}, u32[]{:S(2)}) %collective-permute-start.61) | collective-permute-done | bytes 276512 | tf_op jit(solution)/shard_map/ppermute | solution.py:237
  241.3 4.0 %collective-permute-done.65 = bf16[4,120,640]{2,1,0:T(8,128)(2,1)} collective-permute-done((bf16[4,120,640]{2,1,0:T(8,128)(2,1)}, bf16[4,120,640]{2,1,0:T(8,128)(2,1)}, u32[]{:S(2)}, u32[]{:S(2)}) %collective-permute-start.65) | collective-permute-done | bytes 614432 | tf_op jit(solution)/shard_map/ppermute | solution.py:233
  245.3 1.2 fusion.10
  246.7 3.8 %collective-permute-start.68 = (bf16[120,640]{1,0:T(8,128)(2,1)S(1)}, bf16[120,640]{1,0:T(8,128)(2,1)S(1)}, u32[]{:S(2)}, u32[]{:S(2)}) collective-permute-start(bf16[120,640]{1,0:T(8,128)(2,1)S(1)} %get-tuple-element.87), channel_id=1, source_target_pairs={{0,12},{1,13},{2,14},{3,15},{4,0},{5,1},{6,2},{7,3},{8,4},{9,5},{1... | collective-permute-start | bytes 460808 | tf_op jit(solution)/shard_map/ppermute | solution.py:233
  251.6 3.8 %collective-permute-done.66 = bf16[120,640]{1,0:T(8,128)(2,1)S(1)} collective-permute-done((bf16[120,640]{1,0:T(8,128)(2,1)S(1)}, bf16[120,640]{1,0:T(8,128)(2,1)S(1)}, u32[]{:S(2)}, u32[]{:S(2)}) %collective-permute-start.66) | collective-permute-done | bytes 153632 | tf_op jit(solution)/shard_map/ppermute | solution.py:233
  256.0 5.7 %collective-permute-done.67 = bf16[120,640]{1,0:T(8,128)(2,1)S(1)} collective-permute-done((bf16[120,640]{1,0:T(8,128)(2,1)S(1)}, bf16[120,640]{1,0:T(8,128)(2,1)S(1)}, u32[]{:S(2)}, u32[]{:S(2)}) %collective-permute-start.67) | collective-permute-done | bytes 153632 | tf_op jit(solution)/shard_map/ppermute | solution.py:233
  (249 shorter events, 45.4 us)
Async XLA Ops:
  0.7 7.5 %collective-permute-start = (bf16[120,640]{1,0:T(8,128)(2,1)}, bf16[120,640]{1,0:T(8,128)(2,1)S(1)}, u32[]{:S(2)}, u32[]{:S(2)}) collective-permute-start(bf16[120,640]{1,0:T(8,128)(2,1)} %bitcast.305), channel_id=1, source_target_pairs={{0,4},{1,5},{2,6},{3,7},{4,0},{5,1},{6,2},{7,3},{8,12},{9,13},{10,... | collective-permute-start | bytes 460808 | tf_op jit(solution)/shard_map/ppermute | solution.py:269
  5.6 8.1 %collective-permute-start.8 = (bf16[360,384]{1,0:T(8,128)(2,1)S(1)}, bf16[360,384]{1,0:T(8,128)(2,1)S(1)}, u32[]{:S(2)}, u32[]{:S(2)}) collective-permute-start(bf16[360,384]{1,0:T(8,128)(2,1)S(1)} %pad_maximum_fusion.6), channel_id=1, source_target_pairs={{0,16},{16,0},{1,17},{17,1},{2,18},{18,2},{3,19},{19,3},{4,20},{20... | collective-permute-start | bytes 829448 | tf_op jit(solution)/shard_map/ppermute | solution.py:237
  9.3 44.0 %collective-permute-start.4 = (bf16[2,120,640]{2,1,0:T(8,128)(2,1)S(1)}, bf16[2,120,640]{2,1,0:T(8,128)(2,1)S(1)}, u32[]{:S(2)}, u32[]{:S(2)}) collective-permute-start(bf16[2,120,640]{2,1,0:T(8,128)(2,1)S(1)} %maximum_select_fusion.32), channel_id=1, source_target_pairs={{0,2},{1,3},{2,0},{3,1},{4,6},{5,7},{6,4},{7,5},{8,10},{9,11},{10,... | collective-permute-start | bytes 921608 | tf_op jit(solution)/shard_map/ppermute | solution.py:233
  10.8 10.8 %collective-permute-start.1 = (bf16[2,120,640]{2,1,0:T(8,128)(2,1)S(1)}, bf16[2,120,640]{2,1,0:T(8,128)(2,1)S(1)}, u32[]{:S(2)}, u32[]{:S(2)}) collective-permute-start(bf16[2,120,640]{2,1,0:T(8,128)(2,1)S(1)} %maximum_select_fusion.32), channel_id=1, source_target_pairs={{4,8},{5,9},{6,10},{7,11},{8,4},{9,5},{10,6},{11,7},{20,24},{21,25... | collective-permute-start | bytes 921608 | tf_op jit(solution)/shard_map/ppermute | solution.py:269
  20.9 5.6 %collective-permute-start.10 = (bf16[2,360,128]{2,1,0:T(8,128)(2,1)S(1)}, bf16[2,360,128]{2,1,0:T(8,128)(2,1)S(1)}, u32[]{:S(2)}, u32[]{:S(2)}) collective-permute-start(bf16[2,360,128]{2,1,0:T(8,128)(2,1)S(1)} %maximum_select_fusion.33), channel_id=1, source_target_pairs={{4,8},{5,9},{6,10},{7,11},{8,4},{9,5},{10,6},{11,7},{20,24},{21,25... | collective-permute-start | bytes 552968 | tf_op jit(solution)/shard_map/ppermute | solution.py:269
  21.6 29.8 %collective-permute-start.2 = (bf16[2,120,640]{2,1,0:T(8,128)(2,1)S(1)}, bf16[2,120,640]{2,1,0:T(8,128)(2,1)S(1)}, u32[]{:S(2)}, u32[]{:S(2)}) collective-permute-start(bf16[2,120,640]{2,1,0:T(8,128)(2,1)S(1)} %collective-permute-done.1), channel_id=1, source_target_pairs={{4,0},{5,1},{6,2},{7,3},{8,12},{9,13},{10,14},{11,15},{20,16},{21,... | collective-permute-start | bytes 921608 | tf_op jit(solution)/shard_map/ppermute | solution.py:269
  23.4 11.9 %collective-permute-start.19 = (bf16[360,128]{1,0:T(8,128)(2,1)S(1)}, bf16[360,128]{1,0:T(8,128)(2,1)S(1)}, u32[]{:S(2)}, u32[]{:S(2)}) collective-permute-start(bf16[360,128]{1,0:T(8,128)(2,1)S(1)} %slice_select_fusion.3), channel_id=1, source_target_pairs={{0,4},{1,5},{2,6},{3,7},{4,0},{5,1},{6,2},{7,3},{8,12},{9,13},{10,... | collective-permute-start | bytes 276488 | tf_op jit(solution)/shard_map/ppermute | solution.py:269
  25.7 9.6 %collective-permute-start.15 = (bf16[2,360,128]{2,1,0:T(8,128)(2,1)S(1)}, bf16[2,360,128]{2,1,0:T(8,128)(2,1)S(1)}, u32[]{:S(2)}, u32[]{:S(2)}) collective-permute-start(bf16[2,360,128]{2,1,0:T(8,128)(2,1)S(1)} %maximum_select_fusion.34), channel_id=1, source_target_pairs={{4,8},{5,9},{6,10},{7,11},{8,4},{9,5},{10,6},{11,7},{20,24},{21,25... | collective-permute-start | bytes 552968 | tf_op jit(solution)/shard_map/ppermute | solution.py:269
  26.4 15.2 %collective-permute-start.11 = (bf16[2,360,128]{2,1,0:T(8,128)(2,1)S(1)}, bf16[2,360,128]{2,1,0:T(8,128)(2,1)S(1)}, u32[]{:S(2)}, u32[]{:S(2)}) collective-permute-start(bf16[2,360,128]{2,1,0:T(8,128)(2,1)S(1)} %collective-permute-done.10), channel_id=1, source_target_pairs={{4,0},{5,1},{6,2},{7,3},{8,12},{9,13},{10,14},{11,15},{20,16},{21,... | collective-permute-start | bytes 552968 | tf_op jit(solution)/shard_map/ppermute | solution.py:269
  35.2 5.1 %collective-permute-start.25 = (bf16[360,128]{1,0:T(8,128)(2,1)S(1)}, bf16[360,128]{1,0:T(8,128)(2,1)S(1)}, u32[]{:S(2)}, u32[]{:S(2)}) collective-permute-start(bf16[360,128]{1,0:T(8,128)(2,1)S(1)} %get-tuple-element.35), channel_id=1, source_target_pairs={{0,4},{1,5},{2,6},{3,7},{4,0},{5,1},{6,2},{7,3},{8,12},{9,13},{10,... | collective-permute-start | bytes 276488 | tf_op jit(solution)/shard_map/ppermute | solution.py:269
  35.3 14.1 %collective-permute-start.20 = (bf16[2,360,128]{2,1,0:T(8,128)(2,1)S(1)}, bf16[2,360,128]{2,1,0:T(8,128)(2,1)S(1)}, u32[]{:S(2)}, u32[]{:S(2)}) collective-permute-start(bf16[2,360,128]{2,1,0:T(8,128)(2,1)S(1)} %maximum_select_fusion.35), channel_id=1, source_target_pairs={{4,8},{5,9},{6,10},{7,11},{8,4},{9,5},{10,6},{11,7},{20,24},{21,25... | collective-permute-start | bytes 552968 | tf_op jit(solution)/shard_map/ppermute | solution.py:269
  40.3 12.6 %collective-permute-start.16 = (bf16[2,360,128]{2,1,0:T(8,128)(2,1)S(1)}, bf16[2,360,128]{2,1,0:T(8,128)(2,1)S(1)}, u32[]{:S(2)}, u32[]{:S(2)}) collective-permute-start(bf16[2,360,128]{2,1,0:T(8,128)(2,1)S(1)} %collective-permute-done.15), channel_id=1, source_target_pairs={{4,0},{5,1},{6,2},{7,3},{8,12},{9,13},{10,14},{11,15},{20,16},{21,... | collective-permute-start | bytes 552968 | tf_op jit(solution)/shard_map/ppermute | solution.py:269
  41.7 7.0 %collective-permute-start.30 = (bf16[360,128]{1,0:T(8,128)(2,1)S(1)}, bf16[360,128]{1,0:T(8,128)(2,1)S(1)}, u32[]{:S(2)}, u32[]{:S(2)}) collective-permute-start(bf16[360,128]{1,0:T(8,128)(2,1)S(1)} %get-tuple-element.37), channel_id=1, source_target_pairs={{0,4},{1,5},{2,6},{3,7},{4,0},{5,1},{6,2},{7,3},{8,12},{9,13},{10,... | collective-permute-start | bytes 276488 | tf_op jit(solution)/shard_map/ppermute | solution.py:269
  48.7 5.2 %collective-permute-start.26 = (bf16[2,360,128]{2,1,0:T(8,128)(2,1)S(1)}, bf16[2,360,128]{2,1,0:T(8,128)(2,1)S(1)}, u32[]{:S(2)}, u32[]{:S(2)}) collective-permute-start(bf16[2,360,128]{2,1,0:T(8,128)(2,1)S(1)} %maximum_select_fusion.36), channel_id=1, source_target_pairs={{4,8},{5,9},{6,10},{7,11},{8,4},{9,5},{10,6},{11,7},{20,24},{21,25... | collective-permute-start | bytes 552968 | tf_op jit(solution)/shard_map/ppermute | solution.py:269
  49.5 23.1 %collective-permute-start.12 = (bf16[4,360,128]{2,1,0:T(8,128)(2,1)S(1)}, bf16[4,360,128]{2,1,0:T(8,128)(2,1)S(1)}, u32[]{:S(2)}, u32[]{:S(2)}) collective-permute-start(bf16[4,360,128]{2,1,0:T(8,128)(2,1)S(1)} %maximum_select_fusion.22), channel_id=1, source_target_pairs={{0,2},{1,3},{2,0},{3,1},{4,6},{5,7},{6,4},{7,5},{8,10},{9,11},{10,... | collective-permute-start | bytes 1105928 | tf_op jit(solution)/shard_map/ppermute | solution.py:233
  51.4 14.7 %collective-permute-start.21 = (bf16[2,360,128]{2,1,0:T(8,128)(2,1)S(1)}, bf16[2,360,128]{2,1,0:T(8,128)(2,1)S(1)}, u32[]{:S(2)}, u32[]{:S(2)}) collective-permute-start(bf16[2,360,128]{2,1,0:T(8,128)(2,1)S(1)} %collective-permute-done.20), channel_id=1, source_target_pairs={{4,0},{5,1},{6,2},{7,3},{8,12},{9,13},{10,14},{11,15},{20,16},{21,... | collective-permute-start | bytes 552968 | tf_op jit(solution)/shard_map/ppermute | solution.py:269
  52.9 11.5 %collective-permute-start.3 = (bf16[2,120,640]{2,1,0:T(8,128)(2,1)S(1)}, bf16[2,120,640]{2,1,0:T(8,128)(2,1)S(1)}, u32[]{:S(2)}, u32[]{:S(2)}) collective-permute-start(bf16[2,120,640]{2,1,0:T(8,128)(2,1)S(1)} %broadcast_select_fusion.4), channel_id=1, source_target_pairs={{0,2},{1,3},{2,0},{3,1},{4,6},{5,7},{6,4},{7,5},{8,10},{9,11},{10,... | collective-permute-start | bytes 921608 | tf_op jit(solution)/shard_map/ppermute | solution.py:233
  53.2 13.0 %collective-permute-start.31 = (bf16[2,360,128]{2,1,0:T(8,128)(2,1)S(1)}, bf16[2,360,128]{2,1,0:T(8,128)(2,1)S(1)}, u32[]{:S(2)}, u32[]{:S(2)}) collective-permute-start(bf16[2,360,128]{2,1,0:T(8,128)(2,1)S(1)} %maximum_select_fusion.37), channel_id=1, source_target_pairs={{4,8},{5,9},{6,10},{7,11},{8,4},{9,5},{10,6},{11,7},{20,24},{21,25... | collective-permute-start | bytes 552968 | tf_op jit(solution)/shard_map/ppermute | solution.py:269
  53.9 23.5 %collective-permute-start.17 = (bf16[4,360,128]{2,1,0:T(8,128)(2,1)S(1)}, bf16[4,360,128]{2,1,0:T(8,128)(2,1)S(1)}, u32[]{:S(2)}, u32[]{:S(2)}) collective-permute-start(bf16[4,360,128]{2,1,0:T(8,128)(2,1)S(1)} %maximum_select_fusion.24), channel_id=1, source_target_pairs={{0,2},{1,3},{2,0},{3,1},{4,6},{5,7},{6,4},{7,5},{8,10},{9,11},{10,... | collective-permute-start | bytes 1105928 | tf_op jit(solution)/shard_map/ppermute | solution.py:233
  64.4 7.7 %collective-permute-start.27 = (bf16[2,360,128]{2,1,0:T(8,128)(2,1)S(1)}, bf16[2,360,128]{2,1,0:T(8,128)(2,1)S(1)}, u32[]{:S(2)}, u32[]{:S(2)}) collective-permute-start(bf16[2,360,128]{2,1,0:T(8,128)(2,1)S(1)} %collective-permute-done.26), channel_id=1, source_target_pairs={{4,0},{5,1},{6,2},{7,3},{8,12},{9,13},{10,14},{11,15},{20,16},{21,... | collective-permute-start | bytes 552968 | tf_op jit(solution)/shard_map/ppermute | solution.py:269
  66.1 8.2 %collective-permute-start.5 = (bf16[4,2,120,640]{3,2,0,1:T(8,128)(2,1)S(1)}, bf16[4,2,120,640]{3,2,0,1:T(8,128)(2,1)S(1)}, u32[]{:S(2)}, u32[]{:S(2)}) collective-permute-start(bf16[4,2,120,640]{3,2,0,1:T(8,128)(2,1)S(1)} %maximum_select_fusion.8), channel_id=1, source_target_pairs={{0,1},{1,0},{2,3},{3,2},{4,5},{5,4},{6,7},{7,6},{8,9},{9,8},{10,11... | collective-permute-start | bytes 3686408 | tf_op jit(solution)/shard_map/ppermute | solution.py:233
  66.3 11.1 %collective-permute-start.32 = (bf16[2,360,128]{2,1,0:T(8,128)(2,1)S(1)}, bf16[2,360,128]{2,1,0:T(8,128)(2,1)S(1)}, u32[]{:S(2)}, u32[]{:S(2)}) collective-permute-start(bf16[2,360,128]{2,1,0:T(8,128)(2,1)S(1)} %collective-permute-done.31), channel_id=1, source_target_pairs={{4,0},{5,1},{6,2},{7,3},{8,12},{9,13},{10,14},{11,15},{20,16},{21,... | collective-permute-start | bytes 552968 | tf_op jit(solution)/shard_map/ppermute | solution.py:269
  72.6 7.6 %collective-permute-start.22 = (bf16[4,360,128]{2,1,0:T(8,128)(2,1)S(1)}, bf16[4,360,128]{2,1,0:T(8,128)(2,1)S(1)}, u32[]{:S(2)}, u32[]{:S(2)}) collective-permute-start(bf16[4,360,128]{2,1,0:T(8,128)(2,1)S(1)} %maximum_select_fusion.26), channel_id=1, source_target_pairs={{0,2},{1,3},{2,0},{3,1},{4,6},{5,7},{6,4},{7,5},{8,10},{9,11},{10,... | collective-permute-start | bytes 1105928 | tf_op jit(solution)/shard_map/ppermute | solution.py:233
  74.2 20.8 %collective-permute-start.13 = (bf16[4,2,360,128]{3,2,0,1:T(8,128)(2,1)S(1)}, bf16[4,2,360,128]{3,2,0,1:T(8,128)(2,1)S(1)}, u32[]{:S(2)}, u32[]{:S(2)}) collective-permute-start(bf16[4,2,360,128]{3,2,0,1:T(8,128)(2,1)S(1)} %maximum_select_fusion.10), channel_id=1, source_target_pairs={{0,1},{1,0},{2,3},{3,2},{4,5},{5,4},{6,7},{7,6},{8,9},{9,8},{10,11... | collective-permute-start | bytes 2211848 | tf_op jit(solution)/shard_map/ppermute | solution.py:233
  75.8 19.0 %collective-permute-start.6 = (bf16[576,640]{1,0:T(8,128)(2,1)S(1)}, bf16[576,640]{1,0:T(8,128)(2,1)S(1)}, u32[]{:S(2)}, u32[]{:S(2)}) collective-permute-start(bf16[576,640]{1,0:T(8,128)(2,1)S(1)} %dynamic-slice_bitcast_fusion), channel_id=1, source_target_pairs={{0,16},{16,0},{1,17},{17,1},{2,18},{18,2},{3,19},{19,3},{4,20},{20... | collective-permute-start | bytes 2211848 | tf_op jit(solution)/shard_map/ppermute | solution.py:237
  77.5 10.8 %collective-permute-start.28 = (bf16[4,360,128]{2,1,0:T(8,128)(2,1)S(1)}, bf16[4,360,128]{2,1,0:T(8,128)(2,1)S(1)}, u32[]{:S(2)}, u32[]{:S(2)}) collective-permute-start(bf16[4,360,128]{2,1,0:T(8,128)(2,1)S(1)} %maximum_select_fusion.28), channel_id=1, source_target_pairs={{0,2},{1,3},{2,0},{3,1},{4,6},{5,7},{6,4},{7,5},{8,10},{9,11},{10,... | collective-permute-start | bytes 1105928 | tf_op jit(solution)/shard_map/ppermute | solution.py:233
  78.2 20.2 %collective-permute-start.18 = (bf16[4,2,360,128]{3,2,0,1:T(8,128)(2,1)S(1)}, bf16[4,2,360,128]{3,2,0,1:T(8,128)(2,1)S(1)}, u32[]{:S(2)}, u32[]{:S(2)}) collective-permute-start(bf16[4,2,360,128]{3,2,0,1:T(8,128)(2,1)S(1)} %maximum_select_fusion.12), channel_id=1, source_target_pairs={{0,1},{1,0},{2,3},{3,2},{4,5},{5,4},{6,7},{7,6},{8,9},{9,8},{10,11... | collective-permute-start | bytes 2211848 | tf_op jit(solution)/shard_map/ppermute | solution.py:233
  80.3 18.4 %collective-permute-start.23 = (bf16[4,2,360,128]{3,2,0,1:T(8,128)(2,1)S(1)}, bf16[4,2,360,128]{3,2,0,1:T(8,128)(2,1)S(1)}, u32[]{:S(2)}, u32[]{:S(2)}) collective-permute-start(bf16[4,2,360,128]{3,2,0,1:T(8,128)(2,1)S(1)} %maximum_select_fusion.14), channel_id=1, source_target_pairs={{0,1},{1,0},{2,3},{3,2},{4,5},{5,4},{6,7},{7,6},{8,9},{9,8},{10,11... | collective-permute-start | bytes 2211848 | tf_op jit(solution)/shard_map/ppermute | solution.py:233
  88.3 9.9 %collective-permute-start.33 = (bf16[4,360,128]{2,1,0:T(8,128)(2,1)S(1)}, bf16[4,360,128]{2,1,0:T(8,128)(2,1)S(1)}, u32[]{:S(2)}, u32[]{:S(2)}) collective-permute-start(bf16[4,360,128]{2,1,0:T(8,128)(2,1)S(1)} %maximum_select_fusion.30), channel_id=1, source_target_pairs={{0,2},{1,3},{2,0},{3,1},{4,6},{5,7},{6,4},{7,5},{8,10},{9,11},{10,... | collective-permute-start | bytes 1105928 | tf_op jit(solution)/shard_map/ppermute | solution.py:233
  95.0 13.0 %collective-permute-start.29 = (bf16[4,2,360,128]{3,2,0,1:T(8,128)(2,1)S(1)}, bf16[4,2,360,128]{3,2,0,1:T(8,128)(2,1)S(1)}, u32[]{:S(2)}, u32[]{:S(2)}) collective-permute-start(bf16[4,2,360,128]{3,2,0,1:T(8,128)(2,1)S(1)} %maximum_select_fusion.16), channel_id=1, source_target_pairs={{0,1},{1,0},{2,3},{3,2},{4,5},{5,4},{6,7},{7,6},{8,9},{9,8},{10,11... | collective-permute-start | bytes 2211848 | tf_op jit(solution)/shard_map/ppermute | solution.py:233
  98.3 10.1 %collective-permute-start.34 = (bf16[4,2,360,128]{3,2,0,1:T(8,128)(2,1)S(1)}, bf16[4,2,360,128]{3,2,0,1:T(8,128)(2,1)S(1)}, u32[]{:S(2)}, u32[]{:S(2)}) collective-permute-start(bf16[4,2,360,128]{3,2,0,1:T(8,128)(2,1)S(1)} %maximum_select_fusion.18), channel_id=1, source_target_pairs={{0,1},{1,0},{2,3},{3,2},{4,5},{5,4},{6,7},{7,6},{8,9},{9,8},{10,11... | collective-permute-start | bytes 2211848 | tf_op jit(solution)/shard_map/ppermute | solution.py:233
  106.3 16.3 %collective-permute-start.24 = (bf16[480,640]{1,0:T(8,128)(2,1)S(1)}, bf16[480,640]{1,0:T(8,128)(2,1)S(1)}, u32[]{:S(2)}, u32[]{:S(2)}) collective-permute-start(bf16[480,640]{1,0:T(8,128)(2,1)S(1)} %get-tuple-element.34.own_ref), channel_id=1, source_target_pairs={{0,16},{16,0},{1,17},{17,1},{2,18},{18,2},{3,19},{19,3},{4,20},{20... | collective-permute-start | bytes 1843208 | tf_op jit(solution)/shard_map/ppermute | solution.py:237
  134.5 15.5 %collective-permute-start.35 = (bf16[480,640]{1,0:T(8,128)(2,1)S(1)}, bf16[480,640]{1,0:T(8,128)(2,1)S(1)}, u32[]{:S(2)}, u32[]{:S(2)}) collective-permute-start(bf16[480,640]{1,0:T(8,128)(2,1)S(1)} %get-tuple-element.40.own_ref), channel_id=1, source_target_pairs={{0,16},{16,0},{1,17},{17,1},{2,18},{18,2},{3,19},{19,3},{4,20},{20... | collective-permute-start | bytes 1843208 | tf_op jit(solution)/shard_map/ppermute | solution.py:237
  157.0 7.3 %collective-permute-start.36 = (bf16[4,2,360,128]{3,2,0,1:T(8,128)(2,1)S(1)}, bf16[4,2,360,128]{3,2,0,1:T(8,128)(2,1)S(1)}, u32[]{:S(2)}, u32[]{:S(2)}) collective-permute-start(bf16[4,2,360,128]{3,2,0,1:T(8,128)(2,1)S(1)} %bitcast.294), channel_id=1, source_target_pairs={{0,1},{1,0},{2,3},{3,2},{4,5},{5,4},{6,7},{7,6},{8,9},{9,8},{10,11... | collective-permute-start | bytes 2211848 | tf_op jit(solution)/shard_map/ppermute | solution.py:233
  158.3 7.1 %collective-permute-start.44 = (bf16[4,2,360,128]{3,2,0,1:T(8,128)(2,1)S(1)}, bf16[4,2,360,128]{3,2,0,1:T(8,128)(2,1)S(1)}, u32[]{:S(2)}, u32[]{:S(2)}) collective-permute-start(bf16[4,2,360,128]{3,2,0,1:T(8,128)(2,1)S(1)} %bitcast.297), channel_id=1, source_target_pairs={{0,1},{1,0},{2,3},{3,2},{4,5},{5,4},{6,7},{7,6},{8,9},{9,8},{10,11... | collective-permute-start | bytes 2211848 | tf_op jit(solution)/shard_map/ppermute | solution.py:233
  159.4 6.3 %collective-permute-start.43 = (bf16[4,2,360,128]{3,2,0,1:T(8,128)(2,1)S(1)}, bf16[4,2,360,128]{3,2,0,1:T(8,128)(2,1)S(1)}, u32[]{:S(2)}, u32[]{:S(2)}) collective-permute-start(bf16[4,2,360,128]{3,2,0,1:T(8,128)(2,1)S(1)} %bitcast.293), channel_id=1, source_target_pairs={{0,1},{1,0},{2,3},{3,2},{4,5},{5,4},{6,7},{7,6},{8,9},{9,8},{10,11... | collective-permute-start | bytes 2211848 | tf_op jit(solution)/shard_map/ppermute | solution.py:233
  161.7 20.7 %collective-permute-start.62 = (bf16[2,576,640]{2,1,0:T(8,128)(2,1)S(1)}, bf16[2,576,640]{2,1,0:T(8,128)(2,1)S(1)}, u32[]{:S(2)}, u32[]{:S(2)}) collective-permute-start(bf16[2,576,640]{2,1,0:T(8,128)(2,1)S(1)} %fusion.2), channel_id=1, source_target_pairs={{0,1},{1,0},{2,3},{3,2},{4,5},{5,4},{6,7},{7,6},{8,9},{9,8},{10,11... | collective-permute-start | bytes 4423688 | tf_op jit(solution)/shard_map/ppermute | solution.py:233
  162.8 11.4 %collective-permute-start.46 = (bf16[4,360,128]{2,1,0:T(8,128)(2,1)S(1)}, bf16[4,360,128]{2,1,0:T(8,128)(2,1)S(1)}, u32[]{:S(2)}, u32[]{:S(2)}) collective-permute-start(bf16[4,360,128]{2,1,0:T(8,128)(2,1)S(1)} %dynamic-slice_bitcast_fusion.2), channel_id=1, source_target_pairs={{0,2},{1,3},{2,0},{3,1},{4,6},{5,7},{6,4},{7,5},{8,10},{9,11},{10,... | collective-permute-start | bytes 1105928 | tf_op jit(solution)/shard_map/ppermute | solution.py:233
  164.3 17.2 %collective-permute-start.38 = (bf16[4,360,128]{2,1,0:T(8,128)(2,1)S(1)}, bf16[4,360,128]{2,1,0:T(8,128)(2,1)S(1)}, u32[]{:S(2)}, u32[]{:S(2)}) collective-permute-start(bf16[4,360,128]{2,1,0:T(8,128)(2,1)S(1)} %dynamic-slice_bitcast_fusion.5), channel_id=1, source_target_pairs={{0,2},{1,3},{2,0},{3,1},{4,6},{5,7},{6,4},{7,5},{8,10},{9,11},{10,... | collective-permute-start | bytes 1105928 | tf_op jit(solution)/shard_map/ppermute | solution.py:233
  174.4 11.8 %collective-permute-start.52 = (bf16[360,128]{1,0:T(8,128)(2,1)S(1)}, bf16[360,128]{1,0:T(8,128)(2,1)S(1)}, u32[]{:S(2)}, u32[]{:S(2)}) collective-permute-start(bf16[360,128]{1,0:T(8,128)(2,1)S(1)} %get-tuple-element.97), channel_id=1, source_target_pairs={{0,4},{1,5},{2,6},{3,7},{4,8},{5,9},{6,10},{7,11},{8,12},{9,13},{1... | collective-permute-start | bytes 276488 | tf_op jit(solution)/shard_map/ppermute | solution.py:233
  175.1 11.1 %collective-permute-start.54 = (bf16[360,128]{1,0:T(8,128)(2,1)S(1)}, bf16[360,128]{1,0:T(8,128)(2,1)S(1)}, u32[]{:S(2)}, u32[]{:S(2)}) collective-permute-start(bf16[360,128]{1,0:T(8,128)(2,1)S(1)} %get-tuple-element.98), channel_id=1, source_target_pairs={{0,12},{1,13},{2,14},{3,15},{4,0},{5,1},{6,2},{7,3},{8,4},{9,5},{1... | collective-permute-start | bytes 276488 | tf_op jit(solution)/shard_map/ppermute | solution.py:233
  178.2 9.3 %collective-permute-start.53 = (bf16[360,128]{1,0:T(8,128)(2,1)S(1)}, bf16[360,128]{1,0:T(8,128)(2,1)S(1)}, u32[]{:S(2)}, u32[]{:S(2)}) collective-permute-start(bf16[360,128]{1,0:T(8,128)(2,1)S(1)} %get-tuple-element.99), channel_id=1, source_target_pairs={{0,8},{1,9},{2,10},{3,11},{4,12},{5,13},{6,14},{7,15},{8,0},{9,1},... | collective-permute-start | bytes 276488 | tf_op jit(solution)/shard_map/ppermute | solution.py:233
  181.7 7.5 %collective-permute-start.55 = (bf16[360,128]{1,0:T(8,128)(2,1)S(1)}, bf16[360,128]{1,0:T(8,128)(2,1)S(1)}, u32[]{:S(2)}, u32[]{:S(2)}) collective-permute-start(bf16[360,128]{1,0:T(8,128)(2,1)S(1)} %get-tuple-element.100), channel_id=1, source_target_pairs={{0,4},{1,5},{2,6},{3,7},{4,8},{5,9},{6,10},{7,11},{8,12},{9,13},{1... | collective-permute-start | bytes 276488 | tf_op jit(solution)/shard_map/ppermute | solution.py:233
  182.4 8.0 %collective-permute-start.57 = (bf16[360,128]{1,0:T(8,128)(2,1)S(1)}, bf16[360,128]{1,0:T(8,128)(2,1)S(1)}, u32[]{:S(2)}, u32[]{:S(2)}) collective-permute-start(bf16[360,128]{1,0:T(8,128)(2,1)S(1)} %get-tuple-element.101), channel_id=1, source_target_pairs={{0,12},{1,13},{2,14},{3,15},{4,0},{5,1},{6,2},{7,3},{8,4},{9,5},{1... | collective-permute-start | bytes 276488 | tf_op jit(solution)/shard_map/ppermute | solution.py:233
  186.1 6.8 %collective-permute-start.56 = (bf16[360,128]{1,0:T(8,128)(2,1)S(1)}, bf16[360,128]{1,0:T(8,128)(2,1)S(1)}, u32[]{:S(2)}, u32[]{:S(2)}) collective-permute-start(bf16[360,128]{1,0:T(8,128)(2,1)S(1)} %get-tuple-element.102), channel_id=1, source_target_pairs={{0,8},{1,9},{2,10},{3,11},{4,12},{5,13},{6,14},{7,15},{8,0},{9,1},... | collective-permute-start | bytes 276488 | tf_op jit(solution)/shard_map/ppermute | solution.py:233
  186.2 11.6 %collective-permute-start.39 = (bf16[4,360,128]{2,1,0:T(8,128)(2,1)S(1)}, bf16[4,360,128]{2,1,0:T(8,128)(2,1)S(1)}, u32[]{:S(2)}, u32[]{:S(2)}) collective-permute-start(bf16[4,360,128]{2,1,0:T(8,128)(2,1)S(1)} %dynamic-slice_bitcast_fusion.6), channel_id=1, source_target_pairs={{0,2},{1,3},{2,0},{3,1},{4,6},{5,7},{6,4},{7,5},{8,10},{9,11},{10,... | collective-permute-start | bytes 1105928 | tf_op jit(solution)/shard_map/ppermute | solution.py:233
  187.6 17.4 %collective-permute-start.63 = (bf16[576,640]{1,0:T(8,128)(2,1)S(1)}, bf16[576,640]{1,0:T(8,128)(2,1)S(1)}, u32[]{:S(2)}, u32[]{:S(2)}) collective-permute-start(bf16[576,640]{1,0:T(8,128)(2,1)S(1)} %get-tuple-element.71), channel_id=1, source_target_pairs={{0,16},{16,0},{1,17},{17,1},{2,18},{18,2},{3,19},{19,3},{4,20},{20... | collective-permute-start | bytes 2211848 | tf_op jit(solution)/shard_map/ppermute | solution.py:237
  189.2 14.5 %collective-permute-start.47 = (bf16[4,360,128]{2,1,0:T(8,128)(2,1)S(1)}, bf16[4,360,128]{2,1,0:T(8,128)(2,1)S(1)}, u32[]{:S(2)}, u32[]{:S(2)}) collective-permute-start(bf16[4,360,128]{2,1,0:T(8,128)(2,1)S(1)} %dynamic-slice_bitcast_fusion.3), channel_id=1, source_target_pairs={{0,2},{1,3},{2,0},{3,1},{4,6},{5,7},{6,4},{7,5},{8,10},{9,11},{10,... | collective-permute-start | bytes 1105928 | tf_op jit(solution)/shard_map/ppermute | solution.py:233
  198.0 7.5 %collective-permute-start.40 = (bf16[360,128]{1,0:T(8,128)(2,1)S(1)}, bf16[360,128]{1,0:T(8,128)(2,1)S(1)}, u32[]{:S(2)}, u32[]{:S(2)}) collective-permute-start(bf16[360,128]{1,0:T(8,128)(2,1)S(1)} %get-tuple-element.91), channel_id=1, source_target_pairs={{0,4},{1,5},{2,6},{3,7},{4,8},{5,9},{6,10},{7,11},{8,12},{9,13},{1... | collective-permute-start | bytes 276488 | tf_op jit(solution)/shard_map/ppermute | solution.py:233
  198.7 7.2 %collective-permute-start.42 = (bf16[360,128]{1,0:T(8,128)(2,1)S(1)}, bf16[360,128]{1,0:T(8,128)(2,1)S(1)}, u32[]{:S(2)}, u32[]{:S(2)}) collective-permute-start(bf16[360,128]{1,0:T(8,128)(2,1)S(1)} %get-tuple-element.92), channel_id=1, source_target_pairs={{0,12},{1,13},{2,14},{3,15},{4,0},{5,1},{6,2},{7,3},{8,4},{9,5},{1... | collective-permute-start | bytes 276488 | tf_op jit(solution)/shard_map/ppermute | solution.py:233
  201.8 7.7 %collective-permute-start.41 = (bf16[360,128]{1,0:T(8,128)(2,1)S(1)}, bf16[360,128]{1,0:T(8,128)(2,1)S(1)}, u32[]{:S(2)}, u32[]{:S(2)}) collective-permute-start(bf16[360,128]{1,0:T(8,128)(2,1)S(1)} %get-tuple-element.93), channel_id=1, source_target_pairs={{0,8},{1,9},{2,10},{3,11},{4,12},{5,13},{6,14},{7,15},{8,0},{9,1},... | collective-permute-start | bytes 276488 | tf_op jit(solution)/shard_map/ppermute | solution.py:233
  203.7 8.6 %collective-permute-start.48 = (bf16[4,360,128]{2,1,0:T(8,128)(2,1)S(1)}, bf16[4,360,128]{2,1,0:T(8,128)(2,1)S(1)}, u32[]{:S(2)}, u32[]{:S(2)}) collective-permute-start(bf16[4,360,128]{2,1,0:T(8,128)(2,1)S(1)} %dynamic-slice_bitcast_fusion.4), channel_id=1, source_target_pairs={{0,2},{1,3},{2,0},{3,1},{4,6},{5,7},{6,4},{7,5},{8,10},{9,11},{10,... | collective-permute-start | bytes 1105928 | tf_op jit(solution)/shard_map/ppermute | solution.py:233
  205.2 21.1 %collective-permute-start.64 = (bf16[2,576,640]{2,1,0:T(8,128)(2,1)S(1)}, bf16[2,576,640]{2,1,0:T(8,128)(2,1)S(1)}, u32[]{:S(2)}, u32[]{:S(2)}) collective-permute-start(bf16[2,576,640]{2,1,0:T(8,128)(2,1)S(1)} %get-tuple-element.69), channel_id=1, source_target_pairs={{0,1},{1,0},{2,3},{3,2},{4,5},{5,4},{6,7},{7,6},{8,9},{9,8},{10,11... | collective-permute-start | bytes 4423688 | tf_op jit(solution)/shard_map/ppermute | solution.py:233
  205.4 7.3 %collective-permute-start.58 = (bf16[360,128]{1,0:T(8,128)(2,1)S(1)}, bf16[360,128]{1,0:T(8,128)(2,1)S(1)}, u32[]{:S(2)}, u32[]{:S(2)}) collective-permute-start(bf16[360,128]{1,0:T(8,128)(2,1)S(1)} %get-tuple-element.103), channel_id=1, source_target_pairs={{0,4},{1,5},{2,6},{3,7},{4,8},{5,9},{6,10},{7,11},{8,12},{9,13},{1... | collective-permute-start | bytes 276488 | tf_op jit(solution)/shard_map/ppermute | solution.py:233
  206.0 10.3 %collective-permute-start.60 = (bf16[360,128]{1,0:T(8,128)(2,1)S(1)}, bf16[360,128]{1,0:T(8,128)(2,1)S(1)}, u32[]{:S(2)}, u32[]{:S(2)}) collective-permute-start(bf16[360,128]{1,0:T(8,128)(2,1)S(1)} %get-tuple-element.104), channel_id=1, source_target_pairs={{0,12},{1,13},{2,14},{3,15},{4,0},{5,1},{6,2},{7,3},{8,4},{9,5},{1... | collective-permute-start | bytes 276488 | tf_op jit(solution)/shard_map/ppermute | solution.py:233
  209.5 11.9 %collective-permute-start.59 = (bf16[360,128]{1,0:T(8,128)(2,1)S(1)}, bf16[360,128]{1,0:T(8,128)(2,1)S(1)}, u32[]{:S(2)}, u32[]{:S(2)}) collective-permute-start(bf16[360,128]{1,0:T(8,128)(2,1)S(1)} %get-tuple-element.105), channel_id=1, source_target_pairs={{0,8},{1,9},{2,10},{3,11},{4,12},{5,13},{6,14},{7,15},{8,0},{9,1},... | collective-permute-start | bytes 276488 | tf_op jit(solution)/shard_map/ppermute | solution.py:233
  212.4 9.0 %collective-permute-start.49 = (bf16[360,128]{1,0:T(8,128)(2,1)S(1)}, bf16[360,128]{1,0:T(8,128)(2,1)S(1)}, u32[]{:S(2)}, u32[]{:S(2)}) collective-permute-start(bf16[360,128]{1,0:T(8,128)(2,1)S(1)} %get-tuple-element.94), channel_id=1, source_target_pairs={{0,4},{1,5},{2,6},{3,7},{4,8},{5,9},{6,10},{7,11},{8,12},{9,13},{1... | collective-permute-start | bytes 276488 | tf_op jit(solution)/shard_map/ppermute | solution.py:233
  212.7 8.7 %collective-permute-start.51 = (bf16[360,128]{1,0:T(8,128)(2,1)S(1)}, bf16[360,128]{1,0:T(8,128)(2,1)S(1)}, u32[]{:S(2)}, u32[]{:S(2)}) collective-permute-start(bf16[360,128]{1,0:T(8,128)(2,1)S(1)} %get-tuple-element.95), channel_id=1, source_target_pairs={{0,12},{1,13},{2,14},{3,15},{4,0},{5,1},{6,2},{7,3},{8,4},{9,5},{1... | collective-permute-start | bytes 276488 | tf_op jit(solution)/shard_map/ppermute | solution.py:233
  216.3 9.9 %collective-permute-start.50 = (bf16[360,128]{1,0:T(8,128)(2,1)S(1)}, bf16[360,128]{1,0:T(8,128)(2,1)S(1)}, u32[]{:S(2)}, u32[]{:S(2)}) collective-permute-start(bf16[360,128]{1,0:T(8,128)(2,1)S(1)} %get-tuple-element.96), channel_id=1, source_target_pairs={{0,8},{1,9},{2,10},{3,11},{4,12},{5,13},{6,14},{7,15},{8,0},{9,1},... | collective-permute-start | bytes 276488 | tf_op jit(solution)/shard_map/ppermute | solution.py:233
  229.2 16.1 %collective-permute-start.65 = (bf16[4,120,640]{2,1,0:T(8,128)(2,1)}, bf16[4,120,640]{2,1,0:T(8,128)(2,1)}, u32[]{:S(2)}, u32[]{:S(2)}) collective-permute-start(bf16[4,120,640]{2,1,0:T(8,128)(2,1)} %dynamic-slice_bitcast_fusion.1), channel_id=1, source_target_pairs={{0,2},{1,3},{2,0},{3,1},{4,6},{5,7},{6,4},{7,5},{8,10},{9,11},{10,... | collective-permute-start | bytes 1843208 | tf_op jit(solution)/shard_map/ppermute | solution.py:233
  230.7 8.6 %collective-permute-start.61 = (bf16[360,384]{1,0:T(8,128)(2,1)}, bf16[360,384]{1,0:T(8,128)(2,1)}, u32[]{:S(2)}, u32[]{:S(2)}) collective-permute-start(bf16[360,384]{1,0:T(8,128)(2,1)} %pad_maximum_fusion.7), channel_id=1, source_target_pairs={{0,16},{16,0},{1,17},{17,1},{2,18},{18,2},{3,19},{19,3},{4,20},{20... | collective-permute-start | bytes 829448 | tf_op jit(solution)/shard_map/ppermute | solution.py:237
  246.6 8.8 %collective-permute-start.66 = (bf16[120,640]{1,0:T(8,128)(2,1)S(1)}, bf16[120,640]{1,0:T(8,128)(2,1)S(1)}, u32[]{:S(2)}, u32[]{:S(2)}) collective-permute-start(bf16[120,640]{1,0:T(8,128)(2,1)S(1)} %get-tuple-element.86), channel_id=1, source_target_pairs={{0,4},{1,5},{2,6},{3,7},{4,8},{5,9},{6,10},{7,11},{8,12},{9,13},{1... | collective-permute-start | bytes 460808 | tf_op jit(solution)/shard_map/ppermute | solution.py:233
  246.7 9.3 %collective-permute-start.68 = (bf16[120,640]{1,0:T(8,128)(2,1)S(1)}, bf16[120,640]{1,0:T(8,128)(2,1)S(1)}, u32[]{:S(2)}, u32[]{:S(2)}) collective-permute-start(bf16[120,640]{1,0:T(8,128)(2,1)S(1)} %get-tuple-element.87), channel_id=1, source_target_pairs={{0,12},{1,13},{2,14},{3,15},{4,0},{5,1},{6,2},{7,3},{8,4},{9,5},{1... | collective-permute-start | bytes 460808 | tf_op jit(solution)/shard_map/ppermute | solution.py:233
  250.5 11.1 %collective-permute-start.67 = (bf16[120,640]{1,0:T(8,128)(2,1)S(1)}, bf16[120,640]{1,0:T(8,128)(2,1)S(1)}, u32[]{:S(2)}, u32[]{:S(2)}) collective-permute-start(bf16[120,640]{1,0:T(8,128)(2,1)S(1)} %get-tuple-element.88), channel_id=1, source_target_pairs={{0,8},{1,9},{2,10},{3,11},{4,12},{5,13},{6,14},{7,15},{8,0},{9,1},... | collective-permute-start | bytes 460808 | tf_op jit(solution)/shard_map/ppermute | solution.py:233
  (26 other events, 137.9 us)
